TPU v7x, 32 devices: a whole 2x2x4 slice. The times are simulated.
32 devices in a mesh: expert: 8 (over z, x), shard: 4 (over y, core).
Axes of the slice: x: 2, y: 2, z: 4, core: 2. Of those that a mesh axis runs over, the one named last changes fastest.
Arguments:
- inputs: float32 [8, 1024, 2048], P('expert', 'shard'), may hold values from -6 to 6
- segment_ids: int32 [8, 1024], P('expert'), may hold values from -1 to 1, as said below
- route_ids: int32 [8, 1024, 8], P('expert', 'shard'), may hold values from 0 to 31, all different within a row; in each aligned block of 256 rows (0 to 255, 256 to 511, ..., all dimensions but the last counted through in order) at most 64 rows name the same one
- norm_gains: float32 [4, 2048], P(None, ('expert', 'shard')), may hold values from 0.5 to 1.5
- w_query: float32 [2048, 2048], P(('expert', 'shard')), may hold values from -0.125 to 0.125
- w_key: float32 [2048, 2048], P(('expert', 'shard')), may hold values from -0.125 to 0.125
- w_value: float32 [2048, 2048], P(('expert', 'shard')), may hold values from -0.125 to 0.125
- w_output: float32 [2048, 2048], P(('expert', 'shard')), may hold values from -1 to 1
- w_router: float32 [2048, 32], P(('expert', 'shard')), may hold values from -0.0625 to 0.0625
- experts_gate: float32 [32, 2048, 1024], P('expert', 'shard'), may hold values from -0.125 to 0.125
- experts_up: float32 [32, 2048, 1024], P('expert', 'shard'), may hold values from -0.125 to 0.125
- experts_down: float32 [32, 1024, 2048], P('expert', 'shard'), may hold values from -6 to 6
- cotangent: float32 [8, 1024, 2048], P('expert', 'shard'), may hold values from -6 to 6
Outputs:
- output: float32 [8, 1024, 2048], P('expert', 'shard')
- grad_input: float32 [8, 1024, 2048], P('expert', 'shard')
- grad_gains: float32 [4, 2048], P(None, ('expert', 'shard'))
- grad_query: float32 [2048, 2048], P(('expert', 'shard'))
- grad_key: float32 [2048, 2048], P(('expert', 'shard'))
- grad_value: float32 [2048, 2048], P(('expert', 'shard'))
- grad_output: float32 [2048, 2048], P(('expert', 'shard'))
- grad_router: float32 [2048, 32], P(('expert', 'shard'))
- grad_experts_gate: float32 [32, 2048, 1024], P('expert', 'shard')
- grad_experts_up: float32 [32, 2048, 1024], P('expert', 'shard')
- grad_experts_down: float32 [32, 1024, 2048], P('expert', 'shard')
Inputs may be any that keep to these rules, and one draw needn't show every extreme that they name: `segment_ids`: in each sequence, the tokens 2 j * 256 to (2 j + 2) * 256 - 1 hold exactly one picture piece of 256 consecutive tokens, all with the id j; every other token is text, with the id -1. `route_ids`: each token names 8 different experts. Among the 256 tokens of one device (aligned blocks of 256 tokens) no expert is named more than 64 times, a bound that some block reaches.
All inputs are finite; a program needn't handle non-finite values.
Results may differ from a plain program's by a relative error of at most 0.02.
Values may be sent and summed in bfloat16 or wider, within the bound.
No kernel may reach another device: no remote copies, remote signals or barrier semaphores. Data moves between devices by JAX's collectives and lax.ppermute only.
A program may use at most 448 MiB of HBM per device.

v0:
```python
from functools import partial

import jax
import jax.numpy as jnp
from jax import lax
from jax.sharding import PartitionSpec as P

HEADS = 16
HEAD_DIM = 128
TOP = 8
EXP_DEV = 4


EPSILON = 1e-05
ROPE_BASE = 10000.0


def rms_norm(values, gain_row):
    return (
        values * lax.rsqrt(jnp.mean(values * values, axis=-1, keepdims=True) + EPSILON) * gain_row
    )


def rotate(values, positions):
    half_dim = values.shape[-1] // 2
    frequency = ROPE_BASE ** (-2.0 * jnp.arange(half_dim, dtype=jnp.float32) / values.shape[-1])
    angles = positions.astype(jnp.float32)[:, None] * frequency[None, :]
    cosine = jnp.cos(angles)[:, None, :]
    sine_part = jnp.sin(angles)[:, None, :]
    first_half = values[..., :half_dim]
    second = values[..., half_dim:]
    return jnp.concatenate(
        [first_half * cosine - second * sine_part, second * cosine + first_half * sine_part],
        axis=-1,
    )


def head_norm(raw_rows, gain_row, positions):
    normed_rows = rms_norm(raw_rows, gain_row)
    return rotate(normed_rows.reshape(raw_rows.shape[0], HEADS, HEAD_DIM), positions)


def dot_last(left_side, right_side):
    return lax.dot_general(
        left_side, right_side, (((1,), (1,)), ((), ())), preferred_element_type=jnp.float32
    )


def dot_first(left_side, right_side):
    return lax.dot_general(
        left_side, right_side, (((0,), (0,)), ((), ())), preferred_element_type=jnp.float32
    )


def masked_scores(query_b, keys_heads, allowed):
    scores = jnp.einsum(
        "qhd,khd->hqk", query_b, keys_heads, preferred_element_type=jnp.float32
    ) * HEAD_DIM ** (-0.5)
    return jnp.where(allowed[None], scores, -jnp.inf)


def expert_forward(rows_in, weights_gate, weights_up, weights_down):
    gate_pre = jnp.einsum("erd,edf->erf", rows_in, weights_gate, preferred_element_type=jnp.float32)
    up_pre = jnp.einsum("erd,edf->erf", rows_in, weights_up, preferred_element_type=jnp.float32)
    activation = (jax.nn.silu(gate_pre) * up_pre).astype(jnp.bfloat16)
    rows_out = jnp.einsum(
        "erf,efd->erd", activation, weights_down, preferred_element_type=jnp.float32
    ).astype(jnp.bfloat16)
    return (gate_pre, up_pre, activation, rows_out)


def expert_backward(
    rows_in, grads_in, gate_pre, up_pre, activation, weights_gate, weights_up, weights_down
):
    act_grad = jnp.einsum(
        "erd,efd->erf", grads_in, weights_down, preferred_element_type=jnp.float32
    )
    sigmoid_gate = jax.nn.sigmoid(gate_pre)
    gate_grad = (act_grad * up_pre * sigmoid_gate * (1.0 + gate_pre * (1.0 - sigmoid_gate))).astype(
        jnp.bfloat16
    )
    up_grad = (act_grad * gate_pre * sigmoid_gate).astype(jnp.bfloat16)
    rows_grad = jnp.einsum(
        "erf,edf->erd", gate_grad, weights_gate, preferred_element_type=jnp.float32
    )
    rows_grad = rows_grad + jnp.einsum(
        "erf,edf->erd", up_grad, weights_up, preferred_element_type=jnp.float32
    )
    grad_gate = jnp.einsum("erd,erf->edf", rows_in, gate_grad, preferred_element_type=jnp.float32)
    grad_up = jnp.einsum("erd,erf->edf", rows_in, up_grad, preferred_element_type=jnp.float32)
    grad_down = jnp.einsum("erf,erd->efd", activation, grads_in, preferred_element_type=jnp.float32)
    return (rows_grad.astype(jnp.bfloat16), grad_gate, grad_up, grad_down)


def per_device(
    inputs,
    segment_ids,
    route_ids,
    norm_gains,
    w_query,
    w_key,
    w_value,
    w_output,
    w_router,
    experts_gate,
    experts_up,
    experts_down,
    cotangent,
):
    token_rows = inputs[0]
    out_grad = cotangent[0]
    tok_count = token_rows.shape[0]
    model_width = token_rows.shape[1]
    capacity = tok_count // 4
    expert_ways = lax.axis_size("expert")
    expert_total = w_router.shape[1]
    attention_set = (
        norm_gains.astype(jnp.bfloat16),
        w_query.astype(jnp.bfloat16),
        w_key.astype(jnp.bfloat16),
        w_value.astype(jnp.bfloat16),
        w_output.astype(jnp.bfloat16),
        w_router.astype(jnp.bfloat16),
    )
    gains_low, weight_query, weight_key, weight_value, weight_output, weight_router = (
        lax.all_gather(attention_set[0], ("expert", "shard"), axis=1, tiled=True),
        lax.all_gather(attention_set[1], ("expert", "shard"), axis=0, tiled=True),
        lax.all_gather(attention_set[2], ("expert", "shard"), axis=0, tiled=True),
        lax.all_gather(attention_set[3], ("expert", "shard"), axis=0, tiled=True),
        lax.all_gather(attention_set[4], ("expert", "shard"), axis=0, tiled=True),
        lax.all_gather(attention_set[5], ("expert", "shard"), axis=0, tiled=True),
    )
    gain_attn = gains_low[0].astype(jnp.float32)
    gain_query = gains_low[1].astype(jnp.float32)
    gain_key = gains_low[2].astype(jnp.float32)
    gain_mlp = gains_low[3].astype(jnp.float32)
    normed = rms_norm(token_rows, gain_attn).astype(jnp.bfloat16)
    query_raw = jnp.dot(normed, weight_query, preferred_element_type=jnp.float32)
    key_raw = jnp.dot(normed, weight_key, preferred_element_type=jnp.float32)
    value_rows = jnp.dot(normed, weight_value, preferred_element_type=jnp.float32).astype(
        jnp.bfloat16
    )
    first_row = lax.axis_index("shard") * tok_count
    positions = first_row + jnp.arange(tok_count, dtype=jnp.int32)
    shaper = partial(head_norm, positions=positions)
    query_b = shaper(query_raw, gain_query).astype(jnp.bfloat16)
    key_b = shaper(key_raw, gain_key).astype(jnp.bfloat16)
    keys_all, values_all = (
        lax.all_gather(key_b.reshape(tok_count, model_width), "shard", axis=0, tiled=True),
        lax.all_gather(value_rows, "shard", axis=0, tiled=True),
    )
    seq_len = keys_all.shape[0]
    keys_heads = keys_all.reshape(seq_len, HEADS, HEAD_DIM)
    values_heads = values_all.reshape(seq_len, HEADS, HEAD_DIM)
    all_segments = segment_ids[0]
    own_segments = lax.dynamic_slice_in_dim(all_segments, first_row, tok_count)
    key_positions = jnp.arange(seq_len, dtype=jnp.int32)
    allowed = (key_positions[None, :] <= positions[:, None]) | (
        own_segments[:, None] == all_segments[None, :]
    ) & (own_segments[:, None] >= 0)
    masked = masked_scores(query_b, keys_heads, allowed)
    row_max = jnp.max(masked, axis=-1, keepdims=True)
    log_total = row_max + jnp.log(jnp.sum(jnp.exp(masked - row_max), axis=-1, keepdims=True))
    probs_b = jnp.exp(masked - log_total).astype(jnp.bfloat16)
    attended = (
        jnp.einsum("hqk,khd->qhd", probs_b, values_heads, preferred_element_type=jnp.float32)
        .astype(jnp.bfloat16)
        .reshape(tok_count, model_width)
    )
    hidden = token_rows + jnp.dot(attended, weight_output, preferred_element_type=jnp.float32)
    mlp_in = rms_norm(hidden, gain_mlp).astype(jnp.bfloat16)
    logits = jnp.dot(mlp_in, weight_router, preferred_element_type=jnp.float32)
    router = jax.nn.softmax(logits, axis=-1)
    expert_ids = route_ids[0]
    expert_range = jnp.arange(expert_total, dtype=jnp.int32)
    choose = expert_ids[:, :, None] == expert_range[None, None, :]
    gate_values = jnp.sum(jnp.where(choose, router[:, None, :], 0.0), axis=-1)
    pair_ids = expert_ids.reshape(-1)
    pair_total = pair_ids.shape[0]
    onehot = (pair_ids[:, None] == expert_range[None, :]).astype(jnp.int32)
    rank_index = jnp.sum((jnp.cumsum(onehot, axis=0) - 1) * onehot, axis=1)
    slot_of_pair = (pair_ids % EXP_DEV * expert_ways + pair_ids // EXP_DEV) * capacity + rank_index
    slot_total = expert_total * capacity
    pair_of_slot = (
        jnp.full((slot_total,), -1, jnp.int32)
        .at[slot_of_pair]
        .set(jnp.arange(pair_total, dtype=jnp.int32))
    )
    is_live = (pair_of_slot >= 0)[:, None]
    safe_pair = jnp.maximum(pair_of_slot, 0)
    token_of_slot = safe_pair // TOP
    gate_of_slot = gate_values.reshape(-1)[safe_pair]
    send_shape = (EXP_DEV, expert_ways, capacity, model_width)
    expert_shape = (EXP_DEV, expert_ways * capacity, model_width)
    send_rows = jnp.where(is_live, mlp_in[token_of_slot], jnp.zeros((), jnp.bfloat16)).reshape(
        send_shape
    )
    send_grads = (
        jnp.where(is_live, gate_of_slot[:, None] * out_grad[token_of_slot], 0.0)
        .astype(jnp.bfloat16)
        .reshape(send_shape)
    )
    expert_set = (
        experts_gate.astype(jnp.bfloat16),
        experts_up.astype(jnp.bfloat16),
        experts_down.astype(jnp.bfloat16),
    )
    weights_gate, weights_up, weights_down = (
        lax.all_gather(expert_set[0], "shard", axis=1, tiled=True),
        lax.all_gather(expert_set[1], "shard", axis=1, tiled=True),
        lax.all_gather(expert_set[2], "shard", axis=1, tiled=True),
    )
    received = lax.all_to_all(send_rows, "expert", split_axis=1, concat_axis=1, tiled=True).reshape(
        expert_shape
    )
    gate_pre, up_pre, activation, rows_out = expert_forward(
        received, weights_gate, weights_up, weights_down
    )
    returned = lax.all_to_all(
        rows_out.reshape(send_shape), "expert", split_axis=1, concat_axis=1, tiled=True
    )
    grads_in = lax.all_to_all(
        send_grads, "expert", split_axis=1, concat_axis=1, tiled=True
    ).reshape(expert_shape)
    again_gate, again_up, again_down = (
        lax.all_gather(expert_set[0], "shard", axis=1, tiled=True),
        lax.all_gather(expert_set[1], "shard", axis=1, tiled=True),
        lax.all_gather(expert_set[2], "shard", axis=1, tiled=True),
    )
    rows_grad, grad_gate, grad_up, grad_down = expert_backward(
        received, grads_in, gate_pre, up_pre, activation, again_gate, again_up, again_down
    )
    grads_back = lax.all_to_all(
        rows_grad.reshape(send_shape), "expert", split_axis=1, concat_axis=1, tiled=True
    )
    grad_gate, grad_up, grad_down = (
        lax.psum_scatter(
            grad_gate.astype(jnp.bfloat16), "shard", scatter_dimension=1, tiled=True
        ).astype(jnp.float32),
        lax.psum_scatter(
            grad_up.astype(jnp.bfloat16), "shard", scatter_dimension=1, tiled=True
        ).astype(jnp.float32),
        lax.psum_scatter(
            grad_down.astype(jnp.bfloat16), "shard", scatter_dimension=1, tiled=True
        ).astype(jnp.float32),
    )
    pair_out = (
        returned.reshape(slot_total, model_width)[slot_of_pair]
        .astype(jnp.float32)
        .reshape(tok_count, TOP, model_width)
    )
    pair_grad = (
        grads_back.reshape(slot_total, model_width)[slot_of_pair]
        .astype(jnp.float32)
        .reshape(tok_count, TOP, model_width)
    )
    output = hidden + jnp.sum(gate_values[:, :, None] * pair_out, axis=1)
    gains_low, weight_query, weight_key, weight_value, weight_output, weight_router = (
        lax.all_gather(attention_set[0], ("expert", "shard"), axis=1, tiled=True),
        lax.all_gather(attention_set[1], ("expert", "shard"), axis=0, tiled=True),
        lax.all_gather(attention_set[2], ("expert", "shard"), axis=0, tiled=True),
        lax.all_gather(attention_set[3], ("expert", "shard"), axis=0, tiled=True),
        lax.all_gather(attention_set[4], ("expert", "shard"), axis=0, tiled=True),
        lax.all_gather(attention_set[5], ("expert", "shard"), axis=0, tiled=True),
    )
    gain_attn = gains_low[0].astype(jnp.float32)
    gain_query = gains_low[1].astype(jnp.float32)
    gain_key = gains_low[2].astype(jnp.float32)
    gain_mlp = gains_low[3].astype(jnp.float32)
    gate_grad = jnp.sum(out_grad[:, None, :] * pair_out, axis=-1)
    router_grad = jnp.sum(jnp.where(choose, gate_grad[:, :, None], 0.0), axis=1)
    logit_grad = (
        router * (router_grad - jnp.sum(router * router_grad, axis=-1, keepdims=True))
    ).astype(jnp.bfloat16)
    grad_router = dot_first(mlp_in, logit_grad)
    mlp_in_grad = jnp.sum(pair_grad, axis=1) + dot_last(logit_grad, weight_router)
    unused_mlp, mlp_back = jax.vjp(rms_norm, hidden, gain_mlp)
    hidden_part, gain_mlp_grad = mlp_back(mlp_in_grad)
    hidden_grad = out_grad + hidden_part
    attn_grad = hidden_grad.astype(jnp.bfloat16)
    grad_output = dot_first(attended, attn_grad)
    attended_grad = (
        dot_last(attn_grad, weight_output).astype(jnp.bfloat16).reshape(tok_count, HEADS, HEAD_DIM)
    )
    probs = jnp.exp(masked_scores(query_b, keys_heads, allowed) - log_total)
    probs_grad = jnp.einsum(
        "qhd,khd->hqk", attended_grad, values_heads, preferred_element_type=jnp.float32
    )
    row_delta = jnp.sum(probs * probs_grad, axis=-1, keepdims=True)
    score_grad = (probs * (probs_grad - row_delta)).astype(jnp.bfloat16)
    query_grad = (
        jnp.einsum("hqk,khd->qhd", score_grad, keys_heads, preferred_element_type=jnp.float32)
        * HEAD_DIM ** (-0.5)
    ).astype(jnp.bfloat16)
    key_grad_all = jnp.einsum(
        "hqk,qhd->khd", score_grad, query_b, preferred_element_type=jnp.float32
    ) * HEAD_DIM ** (-0.5)
    value_grad_all = jnp.einsum(
        "hqk,qhd->khd",
        probs.astype(jnp.bfloat16),
        attended_grad,
        preferred_element_type=jnp.float32,
    )
    key_grad, value_grad = (
        lax.psum_scatter(
            key_grad_all.reshape(seq_len, model_width).astype(jnp.bfloat16),
            "shard",
            scatter_dimension=0,
            tiled=True,
        ).astype(jnp.float32),
        lax.psum_scatter(
            value_grad_all.reshape(seq_len, model_width).astype(jnp.bfloat16),
            "shard",
            scatter_dimension=0,
            tiled=True,
        ).astype(jnp.float32),
    )
    unused_query, query_back = jax.vjp(shaper, query_raw, gain_query)
    query_raw_grad, gain_query_grad = query_back(query_grad.astype(jnp.float32))
    key_tokens = (
        key_grad.astype(jnp.bfloat16).astype(jnp.float32).reshape(tok_count, HEADS, HEAD_DIM)
    )
    unused_key, key_back = jax.vjp(shaper, key_raw, gain_key)
    key_raw_grad, gain_key_grad = key_back(key_tokens)
    query_raw_b = query_raw_grad.astype(jnp.bfloat16)
    key_raw_b = key_raw_grad.astype(jnp.bfloat16)
    value_grad_b = value_grad.astype(jnp.bfloat16)
    normed_grad = (
        dot_last(query_raw_b, weight_query)
        + dot_last(key_raw_b, weight_key)
        + dot_last(value_grad_b, weight_value)
    )
    grad_query = dot_first(normed, query_raw_b)
    grad_key = dot_first(normed, key_raw_b)
    grad_value = dot_first(normed, value_grad_b)
    unused_attn, attn_back = jax.vjp(rms_norm, token_rows, gain_attn)
    rows_part, gain_attn_grad = attn_back(normed_grad)
    input_grad = hidden_grad + rows_part
    gain_grads = jnp.stack([gain_attn_grad, gain_query_grad, gain_key_grad, gain_mlp_grad])
    summed = (
        lax.psum_scatter(gain_grads, ("expert", "shard"), scatter_dimension=1, tiled=True),
        lax.psum_scatter(grad_query, ("expert", "shard"), scatter_dimension=0, tiled=True),
        lax.psum_scatter(grad_key, ("expert", "shard"), scatter_dimension=0, tiled=True),
        lax.psum_scatter(grad_value, ("expert", "shard"), scatter_dimension=0, tiled=True),
        lax.psum_scatter(grad_output, ("expert", "shard"), scatter_dimension=0, tiled=True),
        lax.psum_scatter(grad_router, ("expert", "shard"), scatter_dimension=0, tiled=True),
    )
    return (
        output[None],
        input_grad[None],
        summed[0],
        summed[1],
        summed[2],
        summed[3],
        summed[4],
        summed[5],
        grad_gate,
        grad_up,
        grad_down,
    )


def solution(mesh):
    return jax.shard_map(
        per_device,
        mesh=mesh,
        in_specs=(
            P("expert", "shard", None),
            P("expert", None),
            P("expert", "shard", None),
            P(None, ("expert", "shard")),
            P(("expert", "shard"), None),
            P(("expert", "shard"), None),
            P(("expert", "shard"), None),
            P(("expert", "shard"), None),
            P(("expert", "shard"), None),
            P("expert", "shard", None),
            P("expert", "shard", None),
            P("expert", "shard", None),
            P("expert", "shard", None),
        ),
        out_specs=(
            P("expert", "shard", None),
            P("expert", "shard", None),
            P(None, ("expert", "shard")),
            P(("expert", "shard"), None),
            P(("expert", "shard"), None),
            P(("expert", "shard"), None),
            P(("expert", "shard"), None),
            P(("expert", "shard"), None),
            P("expert", "shard", None),
            P("expert", "shard", None),
            P("expert", "shard", None),
        ),
        check_vma=False,
    )
```

profile of v0, /device:TPU:9, one launch (start us, length us, event | category | flops | bytes accessed | tf_op | source)
XLA Modules:
  0.0 2860.5 jit_solution(16770096935486488814)
XLA Ops:
  13.6 35.9 %all-gather = bf16[32,64,4]{1,2,0:T(4,128)(2,1)S(1)} all-gather(bf16[1,64,4]{1,2,0:T(4,128)(2,1)S(1)} %convert_bitcast_fusion.2), channel_id=1, replica_groups=mesh['expert'=8,'shard'=4] {'expert','shard'}, dimensions={0}, use_global_device_ids=true | all-gather | bytes 16896 | tf_op jit(solution)/shard_map/all_gather | solution.py:126
  52.0 38.8 %all-gather.18.cloned.1.call-done = bf16[2048,2048]{1,0:T(8,128)(2,1)} async-done(((bf16[64,2048]{1,0:T(8,128)(2,1)}), bf16[2048,2048]{1,0:T(8,128)(2,1)}) %all-gather.18.cloned.1.call-update) | async-done | bytes 8388624 | tf_op jit(solution)/shard_map/all_gather | solution.py:128
  98.5 71.9 %all-gather.16.cloned.1.call-done = bf16[2048,2048]{1,0:T(8,128)(2,1)} async-done(((bf16[64,2048]{1,0:T(8,128)(2,1)}), bf16[2048,2048]{1,0:T(8,128)(2,1)}) %all-gather.16.cloned.1.call-update) | async-done | bytes 8388624 | tf_op jit(solution)/shard_map/all_gather | solution.py:127
  185.3 64.7 %all-gather.12.cloned.1.call-done = bf16[2048,2048]{1,0:T(8,128)(2,1)} async-done(((bf16[64,2048]{1,0:T(8,128)(2,1)}), bf16[2048,2048]{1,0:T(8,128)(2,1)}) %all-gather.12.cloned.1.call-update) | async-done | bytes 8388624 | tf_op jit(solution)/shard_map/all_gather | solution.py:129
  280.7 34.2 %all-gather.1 = bf16[32,64,32]{1,2,0:T(8,128)(2,1)S(1)} all-gather(bf16[1,64,32]{1,2,0:T(8,128)(2,1)S(1)} %convert_bitcast_fusion.1), channel_id=1, replica_groups=mesh['expert'=8,'shard'=4] {'expert','shard'}, dimensions={0}, use_global_device_ids=true | all-gather | bytes 135168 | tf_op jit(solution)/shard_map/all_gather | solution.py:131
  360.9 43.3 %all-gather.22.cloned.1.call-done = bf16[2048,2048]{1,0:T(8,128)(2,1)} async-done(((bf16[64,2048]{1,0:T(8,128)(2,1)}), bf16[2048,2048]{1,0:T(8,128)(2,1)}) %all-gather.22.cloned.1.call-update) | async-done | bytes 8388624 | tf_op jit(solution)/shard_map/all_gather | solution.py:130
  464.4 156.4 %all-to-all-done.2 = bf16[4,8,64,2048]{3,2,0,1:T(8,128)(2,1)} async-done(((bf16[4,8,64,2048]{3,2,0,1:T(8,128)(2,1)}), bf16[4,8,64,2048]{3,2,0,1:T(8,128)(2,1)}, u32[]{:S(2)}, u32[]{:S(2)}) %all-to-all-start.2) | async-done | bytes 8388640 | tf_op jit(solution)/shard_map/all_to_all | solution.py:222
  638.4 170.3 %all-to-all-done = bf16[4,8,64,2048]{3,2,0,1:T(8,128)(2,1)} async-done(((bf16[4,8,64,2048]{3,2,0,1:T(8,128)(2,1)}), bf16[4,8,64,2048]{3,2,0,1:T(8,128)(2,1)}, u32[]{:S(2)}, u32[]{:S(2)}) %all-to-all-start) | async-done | bytes 8388640 | tf_op jit(solution)/shard_map/all_to_all | solution.py:213
  817.1 16.8 fusion.58
  833.9 16.8 fusion.57
  850.7 22.8 multiply_convert_fusion.2
  873.5 17.7 convolution_convert_fusion.3
  905.1 17.0 fusion.59
  922.1 18.2 add_convert_fusion
  948.7 137.9 %all-to-all-done.1 = bf16[4,8,64,2048]{3,2,0,1:T(8,128)(2,1)} async-done(((bf16[4,8,64,2048]{3,2,0,1:T(8,128)(2,1)}), bf16[4,8,64,2048]{3,2,0,1:T(8,128)(2,1)}, u32[]{:S(2)}, u32[]{:S(2)}) %all-to-all-start.1) | async-done | bytes 8388640 | tf_op jit(solution)/shard_map/all_to_all | solution.py:219
  1100.6 20.9 gather_fusion.1
  1131.1 143.1 %all-to-all-done.3 = bf16[4,8,64,2048]{3,2,0,1:T(8,128)(2,1)} async-done(((bf16[4,8,64,2048]{3,2,0,1:T(8,128)(2,1)}), bf16[4,8,64,2048]{3,2,0,1:T(8,128)(2,1)}, u32[]{:S(2)}, u32[]{:S(2)}) %all-to-all-start.3) | async-done | bytes 8388640 | tf_op jit(solution)/shard_map/all_to_all | solution.py:233
  1282.7 20.9 gather_fusion.4
  1325.4 14.4 multiply_reduce_fusion
  1377.4 25.5 reduce-scatter.16.cloned.1.call-done
  1427.2 22.8 reduce-scatter.18.cloned.1.call-done
  1459.9 16.5 convolution_convert_fusion
  1476.4 15.9 convolution_convert_fusion.1
  1492.6 15.8 convolution_convert_fusion.2
  1568.5 128.1 %reduce-scatter.34.cloned.1.call-done = f32[64,4]{1,0:T(8,128)} async-done(((f32[2048,4]{1,0:T(8,128)}), f32[64,4]{1,0:T(8,128)}) %reduce-scatter.34.cloned.1.call-update) | async-done | bytes 1040
  1698.0 147.1 %reduce-scatter.32.cloned.1.call-done = bf16[4,256,2048]{2,1,0:T(8,128)(2,1)} async-done(((bf16[4,1024,2048]{2,1,0:T(8,128)(2,1)}), bf16[4,256,2048]{2,1,0:T(8,128)(2,1)}) %reduce-scatter.32.cloned.1.call-update) | async-done | bytes 4194320 | tf_op jit(solution)/shard_map/reduce_scatter | solution.py:243
  1851.8 122.1 %reduce-scatter.30.cloned.1.call-done = bf16[4,512,1024]{2,1,0:T(8,128)(2,1)} async-done(((bf16[4,2048,1024]{2,1,0:T(8,128)(2,1)}), bf16[4,512,1024]{2,1,0:T(8,128)(2,1)}) %reduce-scatter.30.cloned.1.call-update) | async-done | bytes 4194320 | tf_op jit(solution)/shard_map/reduce_scatter | solution.py:240
  1980.5 122.0 %reduce-scatter.28.cloned.1.call-done = bf16[4,512,1024]{2,1,0:T(8,128)(2,1)} async-done(((bf16[4,2048,1024]{2,1,0:T(8,128)(2,1)}), bf16[4,512,1024]{2,1,0:T(8,128)(2,1)}) %reduce-scatter.28.cloned.1.call-update) | async-done | bytes 4194320 | tf_op jit(solution)/shard_map/reduce_scatter | solution.py:237
  2109.1 181.7 %reduce-scatter.26.cloned.1.call-done = f32[64,2048]{1,0:T(8,128)} async-done(((f32[2048,2048]{1,0:T(8,128)}), f32[64,2048]{1,0:T(8,128)}) %reduce-scatter.26.cloned.1.call-update) | async-done | bytes 524304 | tf_op jit(solution)/shard_map/reduce_scatter | solution.py:345
  2290.8 187.4 %reduce-scatter.24.cloned.1.call-done = f32[64,2048]{1,0:T(8,128)} async-done(((f32[2048,2048]{1,0:T(8,128)}), f32[64,2048]{1,0:T(8,128)}) %reduce-scatter.24.cloned.1.call-update) | async-done | bytes 524304 | tf_op jit(solution)/shard_map/reduce_scatter | solution.py:344
  2478.2 187.6 %reduce-scatter.22.cloned.1.call-done = f32[64,2048]{1,0:T(8,128)} async-done(((f32[2048,2048]{1,0:T(8,128)}), f32[64,2048]{1,0:T(8,128)}) %reduce-scatter.22.cloned.1.call-update) | async-done | bytes 524304 | tf_op jit(solution)/shard_map/reduce_scatter | solution.py:343
  2665.8 187.4 %reduce-scatter.20.cloned.1.call-done = f32[64,2048]{1,0:T(8,128)} async-done(((f32[2048,2048]{1,0:T(8,128)}), f32[64,2048]{1,0:T(8,128)}) %reduce-scatter.20.cloned.1.call-update) | async-done | bytes 524304 | tf_op jit(solution)/shard_map/reduce_scatter | solution.py:342
  (349 shorter events, 422.8 us)
Async XLA Ops:
  7.2 83.5 %all-gather.18.cloned.1.call-start = ((), (), s32[]{:S(2)}) async-start(), calls=%async_computation.18 | async-start | bytes 8650752 | tf_op jit(solution)/shard_map/all_gather | solution.py:128
  9.2 161.2 %all-gather.16.cloned.1.call-start = ((), (), s32[]{:S(2)}) async-start(), calls=%async_computation.17 | async-start | bytes 8650752 | tf_op jit(solution)/shard_map/all_gather | solution.py:127
  11.0 239.0 %all-gather.12.cloned.1.call-start = ((), (), s32[]{:S(2)}) async-start(), calls=%async_computation.15 | async-start | bytes 8650752 | tf_op jit(solution)/shard_map/all_gather | solution.py:129
  12.9 325.7 %all-gather.20.cloned.1.call-start = ((), (), s32[]{:S(2)}) async-start(), calls=%async_computation.19 | async-start | bytes 5242880 | tf_op jit(solution)/shard_map/all_gather | solution.py:149
  50.4 128.4 %copy-start.28 = (f32[256,64]{1,0:T(8,128)}, f32[256,64]{1,0:T(8,128)S(1)}, u32[]{:S(2)}) copy-start(f32[256,64]{1,0:T(8,128)S(1)} %get-tuple-element.50) | copy-start | bytes 196612
  50.4 128.4 %copy-start.30 = (f32[256,64]{1,0:T(8,128)}, f32[256,64]{1,0:T(8,128)S(1)}, u32[]{:S(2)}) copy-start(f32[256,64]{1,0:T(8,128)S(1)} %get-tuple-element.51) | copy-start | bytes 196612
  51.1 125.1 %copy-start.41 = (f32[1,2048]{1,0:T(1,128)}, f32[1,2048]{1,0:T(1,128)S(1)}, u32[]{:S(2)}) copy-start(f32[1,2048]{1,0:T(1,128)S(1)} %get-tuple-element.46) | copy-start | bytes 24580
  52.0 198.0 %copy-start.16 = (bf16[256,2048]{1,0:T(8,128)(2,1)}, bf16[256,2048]{1,0:T(8,128)(2,1)S(1)}, u32[]{:S(2)}) copy-start(bf16[256,2048]{1,0:T(8,128)(2,1)S(1)} %multiply_convert_fusion.7) | copy-start | bytes 3145732
  184.9 71.9 %copy-start.38 = (f32[64,2048]{1,0:T(8,128)S(1)}, f32[64,2048]{1,0:T(8,128)}, u32[]{:S(2)}) copy-start(f32[64,2048]{1,0:T(8,128)} %param.20) | copy-start | bytes 1572868
  184.9 165.4 %all-gather.14.cloned.1.call-start = ((), (), s32[]{:S(2)}) async-start(), calls=%async_computation.16 | async-start | bytes 5242880 | tf_op jit(solution)/shard_map/all_gather | solution.py:150
  256.7 147.5 %all-gather.22.cloned.1.call-start = ((), (), s32[]{:S(2)}) async-start(), calls=%async_computation.20 | async-start | bytes 8650752 | tf_op jit(solution)/shard_map/all_gather | solution.py:130
  257.5 559.6 %all-gather.26.cloned.1.call-start = ((), (), s32[]{:S(2)}) async-start(), calls=%async_computation.22 | async-start | bytes 20971520 | tf_op jit(solution)/shard_map/all_gather | solution.py:210
  264.3 569.6 %all-gather.24.cloned.1.call-start = ((), (), s32[]{:S(2)}) async-start(), calls=%async_computation.21 | async-start | bytes 20971520 | tf_op jit(solution)/shard_map/all_gather | solution.py:209
  270.4 55.1 %copy-start = (f32[1,256,2048]{2,1,0:T(8,128)S(1)}, f32[1,256,2048]{2,1,0:T(8,128)}, u32[]{:S(2)}) copy-start(f32[1,256,2048]{2,1,0:T(8,128)} %param.25) | copy-start | bytes 6291460
  315.3 96.4 %copy-start.34 = (bf16[2048,32]{0,1:T(8,128)(2,1)}, bf16[2048,32]{0,1:T(8,128)(2,1)S(1)}, u32[]{:S(2)}) copy-start(bf16[2048,32]{0,1:T(8,128)(2,1)S(1)} %reshape.575) | copy-start | bytes 393220
  434.3 186.5 %all-to-all-start.2 = ((bf16[4,8,64,2048]{3,2,0,1:T(8,128)(2,1)}), bf16[4,8,64,2048]{3,2,0,1:T(8,128)(2,1)}, u32[]{:S(2)}, u32[]{:S(2)}) async-start(bf16[4,8,64,2048]{3,2,0,1:T(8,128)(2,1)} %fusion.3), calls=%async_computation.2 | async-start | bytes 16777216 | tf_op jit(solution)/shard_map/all_to_all | solution.py:222
  439.4 411.3 %all-gather.28.cloned.1.call-start = ((), (), s32[]{:S(2)}) async-start(), calls=%async_computation.23 | async-start | bytes 20971520 | tf_op jit(solution)/shard_map/all_gather | solution.py:211
  620.8 187.9 %all-to-all-start = ((bf16[4,8,64,2048]{3,2,0,1:T(8,128)(2,1)}), bf16[4,8,64,2048]{3,2,0,1:T(8,128)(2,1)}, u32[]{:S(2)}, u32[]{:S(2)}) async-start(bf16[4,8,64,2048]{3,2,0,1:T(8,128)(2,1)} %copy_select_fusion), calls=%async_computation | async-start | bytes 16777216 | tf_op jit(solution)/shard_map/all_to_all | solution.py:213
  899.5 187.1 %all-to-all-start.1 = ((bf16[4,8,64,2048]{3,2,0,1:T(8,128)(2,1)}), bf16[4,8,64,2048]{3,2,0,1:T(8,128)(2,1)}, u32[]{:S(2)}, u32[]{:S(2)}) async-start(bf16[4,8,64,2048]{3,2,0,1:T(8,128)(2,1)} %copy.200), calls=%async_computation.1 | async-start | bytes 16777216 | tf_op jit(solution)/shard_map/all_to_all | solution.py:219
  948.7 143.5 %copy-start.56 = (s32[2048,1]{0,1:T(1,128)S(1)}, s32[2048,1]{0,1:T(1,128)}, u32[]{:S(2)}) copy-start(s32[2048,1]{0,1:T(1,128)} %copy-done.55) | copy-start | bytes 24580
  1086.6 187.6 %all-to-all-start.3 = ((bf16[4,8,64,2048]{3,2,0,1:T(8,128)(2,1)}), bf16[4,8,64,2048]{3,2,0,1:T(8,128)(2,1)}, u32[]{:S(2)}, u32[]{:S(2)}) async-start(bf16[4,8,64,2048]{3,2,0,1:T(8,128)(2,1)} %copy.206), calls=%async_computation.3 | async-start | bytes 16777216 | tf_op jit(solution)/shard_map/all_to_all | solution.py:233
  1092.2 310.7 %reduce-scatter.16.cloned.1.call-start = ((), (), s32[]{:S(2)}) async-start(), calls=%async_computation.24 | async-start | bytes 5242880 | tf_op jit(solution)/shard_map/reduce_scatter | solution.py:305
  1357.3 92.8 %reduce-scatter.18.cloned.1.call-start = ((), (), s32[]{:S(2)}) async-start(), calls=%async_computation.25 | async-start | bytes 5242880 | tf_op jit(solution)/shard_map/reduce_scatter | solution.py:311
  1366.9 196.1 %reduce-scatter.36.cloned.1.call-start = ((), (), s32[]{:S(2)}) async-start(), calls=%async_computation.34 | async-start | bytes 1081344
  1376.9 319.7 %reduce-scatter.34.cloned.1.call-start = ((), (), s32[]{:S(2)}) async-start(), calls=%async_computation.33 | async-start | bytes 1081344
  1459.8 385.3 %reduce-scatter.32.cloned.1.call-start = ((), (), s32[]{:S(2)}) async-start(), calls=%async_computation.32 | async-start | bytes 20971520 | tf_op jit(solution)/shard_map/reduce_scatter | solution.py:243
  1476.4 497.5 %reduce-scatter.30.cloned.1.call-start = ((), (), s32[]{:S(2)}) async-start(), calls=%async_computation.31 | async-start | bytes 20971520 | tf_op jit(solution)/shard_map/reduce_scatter | solution.py:240
  1492.3 610.1 %reduce-scatter.28.cloned.1.call-start = ((), (), s32[]{:S(2)}) async-start(), calls=%async_computation.30 | async-start | bytes 20971520 | tf_op jit(solution)/shard_map/reduce_scatter | solution.py:237
  1508.5 782.3 %reduce-scatter.26.cloned.1.call-start = ((), (), s32[]{:S(2)}) async-start(), calls=%async_computation.29 | async-start | bytes 17301504 | tf_op jit(solution)/shard_map/reduce_scatter | solution.py:345
  1519.4 958.8 %reduce-scatter.24.cloned.1.call-start = ((), (), s32[]{:S(2)}) async-start(), calls=%async_computation.28 | async-start | bytes 17301504 | tf_op jit(solution)/shard_map/reduce_scatter | solution.py:344
  1530.1 1135.7 %reduce-scatter.22.cloned.1.call-start = ((), (), s32[]{:S(2)}) async-start(), calls=%async_computation.27 | async-start | bytes 17301504 | tf_op jit(solution)/shard_map/reduce_scatter | solution.py:343
  1539.7 1313.5 %reduce-scatter.20.cloned.1.call-start = ((), (), s32[]{:S(2)}) async-start(), calls=%async_computation.26 | async-start | bytes 17301504 | tf_op jit(solution)/shard_map/reduce_scatter | solution.py:342
  (78 other events, 712.0 us)
Sparse Core Ops, SparseCore 0:
  11.5 79.2 all-gather.17
  94.2 76.1 all-gather.15
  173.8 76.1 all-gather.11
  252.0 33.5 all-gather.19
  287.6 35.5 all-gather.13
  326.4 77.7 all-gather.21
  405.8 104.4 all-gather.25
  511.8 105.9 all-gather.23
  619.4 105.9 all-gather.27
  1357.4 45.4 reduce-scatter.15
  1405.5 44.4 reduce-scatter.17
  1452.2 110.7 reduce-scatter.35
  1565.9 130.6 reduce-scatter.33
  1699.0 146.0 reduce-scatter.31
  1847.7 126.0 reduce-scatter.29
  1976.3 126.1 reduce-scatter.27
  2105.3 185.4 reduce-scatter.25
  2293.6 184.5 reduce-scatter.23
  2481.2 184.5 reduce-scatter.21
  2668.6 184.5 reduce-scatter.19
where the time goes:
time: 2870 us; the launch traced here: 2860 us
  waiting for transfers between devices  2150 us (75%)
  matrix products  294 us (10%)
  local copies, waits for them, and re-layouts  172 us (6%)
  other arithmetic  132 us (5%)
  blocking collectives  70.1 us (2%)
    reduce_scatter x1, waiting for transfers between devices, per_device(): lax.psum_scatter(grad_key, ('expert', 'shard'), scatter_dimension=0, tile...  188 us
    reduce_scatter x1, waiting for transfers between devices, per_device(): lax.psum_scatter(grad_value, ('expert', 'shard'), scatter_dimension=0, ti...  187 us
    reduce_scatter x1, waiting for transfers between devices, per_device(): lax.psum_scatter(grad_query, ('expert', 'shard'), scatter_dimension=0, ti...  187 us
    reduce_scatter x1, waiting for transfers between devices, per_device(): lax.psum_scatter(grad_output, ('expert', 'shard'), scatter_dimension=0, t...  182 us
    all_to_all x1, waiting for transfers between devices, per_device(): lax.all_to_all(send_rows, 'expert', split_axis=1, concat_axis=1, tiled=True)  170 us
    all_to_all x1, waiting for transfers between devices, per_device(): lax.all_to_all(send_grads, 'expert', split_axis=1, concat_axis=1, tiled=T...  156 us
    reduce_scatter x1, waiting for transfers between devices, per_device(): lax.psum_scatter(grad_down.astype(jnp.bfloat16), 'shard', scatter_dimensi...  147 us
    all_to_all x1, waiting for transfers between devices, per_device(): lax.all_to_all(rows_grad.reshape(send_shape), 'expert', split_axis=1, con...  143 us
  transfers between devices with their start and end apart: 24, of which 19 were waited for; matrix products, arithmetic and copies ran while one was open for 16% of the time, Pallas kernels for 0%

commit v1 on v0

v1 whole, which is shorter than its diff:
```python
from functools import partial

import jax
import jax.numpy as jnp
from jax import lax
from jax.experimental import pallas as pl
from jax.experimental.pallas import tpu as pltpu
from jax.sharding import PartitionSpec as P

HEAD_DIM = 128
EXP_DEV = 4
BLOCK = 512
EPSILON = 1e-05
ROPE_BASE = 10000.0
LOW = jnp.bfloat16
F32 = jnp.float32


def inverse_rms(mean_square):
    return lax.rsqrt(mean_square + EPSILON)


def rms_back(values, inverse, gain, grad):
    scaled = gain * grad
    inner = jnp.mean(values * scaled, axis=-1, keepdims=True)
    values_grad = inverse * scaled - values * (inverse * inverse * inverse * inner)
    gain_grad = jnp.sum(grad * values * inverse, axis=0)
    return values_grad, gain_grad


def mm(left, right):
    return jnp.dot(left, right, preferred_element_type=F32)


def dot_last(left, right):
    return lax.dot_general(left, right, (((1,), (1,)), ((), ())), preferred_element_type=F32)


def dot_first(left, right):
    return lax.dot_general(left, right, (((0,), (0,)), ((), ())), preferred_element_type=F32)


def rope_tables(count):
    half = HEAD_DIM // 2
    frequency = ROPE_BASE ** (-2.0 * jnp.arange(half, dtype=F32) / HEAD_DIM)
    angles = jnp.arange(count, dtype=F32)[:, None] * frequency[None, :]
    cosine = jnp.cos(angles)
    sine = jnp.sin(angles)
    return (
        jnp.concatenate([cosine, cosine], axis=-1),
        jnp.concatenate([-sine, sine], axis=-1),
    )


def ring_order(ways):
    return list(range(0, ways, 2)) + list(range(1, ways, 2))[::-1]


def ring_order_inverse(ways):
    order = ring_order(ways)
    return [order.index(i) for i in range(ways)]


def ring_steps(ways):
    order = ring_order(ways)
    forward = [(order[i], order[(i + 1) % ways]) for i in range(ways)]
    return forward, [(b, a) for a, b in forward]


def tie(value, others):
    value, others = lax.optimization_barrier((value, others))
    return value, others


class RingGather:
    def __init__(self, block, ways):
        self.ways, self.done = ways, 0
        self.forward, self.backward = ring_steps(ways)
        self.held = {0: block}

    def step(self):
        ways, far = self.ways, self.ways // 2
        self.done += 1
        step = self.done
        held = self.held
        held[step] = lax.ppermute(held[step - 1], "expert", self.forward)
        if step < ways - far:
            before = held[(ways - step + 1) % ways]
            held[ways - step] = lax.ppermute(before, "expert", self.backward)

    def finish(self):
        while self.done < self.ways // 2:
            self.step()
        return [self.held[i] for i in range(self.ways)]

    def tie(self, value):
        value, self.held = tie(value, self.held)
        return value

    def last(self):
        return self.held[self.done]


class RingScatter:
    def __init__(self, piece, ways):
        self.piece, self.ways = piece, ways
        self.forward, self.backward = ring_steps(ways)
        self.far = ways // 2
        self.near = ways - 1 - self.far
        self.left_step, self.right_step = self.near, self.far
        self.state = (piece(ways - self.far), piece(self.near))

    def add(self, got, index):
        return (got.astype(F32) + self.piece(index).astype(F32)).astype(LOW)

    def step(self):
        right, left = self.state
        if self.right_step == self.left_step:
            left = lax.ppermute(left, "expert", self.backward)
            self.left_step -= 1
            if self.left_step:
                left = self.add(left, self.left_step)
        right = lax.ppermute(right, "expert", self.forward)
        self.right_step -= 1
        if self.right_step:
            right = self.add(right, self.ways - self.right_step)
        self.state = (right, left)

    def finish(self):
        while self.right_step:
            self.step()
        right, left = self.state
        return self.piece(0).astype(F32) + right.astype(F32) + left.astype(F32)

    def tie(self, value):
        value, self.state = tie(value, self.state)
        return value


def flip_steps(shards, distance):
    return [(i, i ^ distance) for i in range(shards)]


class ShardGather:
    def __init__(self, block, shards):
        self.shards, self.distance = shards, shards // 2
        self.held = {0: block}

    def hop(self):
        steps = flip_steps(self.shards, self.distance)
        for key in list(self.held):
            self.held[key ^ self.distance] = lax.ppermute(self.held[key], "shard", steps)
        self.distance //= 2

    def tie(self, value):
        value, self.held = tie(value, self.held)
        return value

    def whole(self, mine):
        while self.distance:
            self.hop()
        size = self.held[0].shape[0]
        shape = (self.shards * size,) + self.held[0].shape[1:]
        whole = jnp.zeros(shape, self.held[0].dtype)
        for key, piece in self.held.items():
            whole = lax.dynamic_update_slice_in_dim(whole, piece, (mine ^ key) * size, 0)
        return whole


class ShardScatter:
    def __init__(self, pieces, shards):
        self.shards, self.distance = shards, 1
        self.held = dict(enumerate(pieces))

    def hop(self, late=None):
        steps = flip_steps(self.shards, self.distance)
        last = 2 * self.distance == self.shards
        for key in list(self.held):
            if key & self.distance:
                got = lax.ppermute(self.held.pop(key), "shard", steps)
                if late is not None:
                    got, _ = tie(got, late)
                rest = self.held[key ^ self.distance].astype(F32) + got.astype(F32)
                self.held[key ^ self.distance] = rest if last else rest.astype(LOW)
        self.distance *= 2

    def finish(self):
        while self.distance < self.shards:
            self.hop()
        return self.held[0]


def shard_pieces(whole, shards, mine):
    size = whole.shape[0] // shards
    return [
        lax.dynamic_slice_in_dim(whole, (mine ^ key) * size, size, 0) for key in range(shards)
    ]


def dispatch_body(ways, *refs):
    pick_ref, sources, out_ref = refs[0], refs[1:-1], refs[-1]
    experts, _, capacity, tokens = pick_ref.shape
    for block in range(ways):
        pick = pick_ref[:, block].reshape(experts * capacity, tokens)
        got = mm(pick, sources[block][...]).astype(LOW)
        out_ref[:, block * capacity : (block + 1) * capacity, :] = got.reshape(
            experts, capacity, got.shape[-1]
        )


def dispatch(pick, blocks):
    experts, ways, capacity, tokens = pick.shape
    width = blocks[0].shape[-1]
    chunk = 512
    return pl.pallas_call(
        partial(dispatch_body, ways),
        grid=(width // chunk,),
        in_specs=[pl.BlockSpec(pick.shape, lambda i: (0, 0, 0, 0))]
        + [pl.BlockSpec((tokens, chunk), lambda i: (0, i))] * ways,
        out_specs=pl.BlockSpec((experts, ways * capacity, chunk), lambda i: (0, 0, i)),
        out_shape=jax.ShapeDtypeStruct((experts, ways * capacity, width), LOW),
        compiler_params=pltpu.CompilerParams(vmem_limit_bytes=48 * 2**20),
        cost_estimate=pl.CostEstimate(
            flops=2 * experts * ways * capacity * tokens * width,
            bytes_accessed=4 * experts * ways * capacity * width,
            transcendentals=0,
        ),
        name="dispatch",
    )(pick, *blocks)


def expert_body(
    places_ref, rows_ref, grads_ref, router_ref, gate, up, down,
    act_ref, gate_out, up_out, pair_ref, weighted_ref, slot_ref,
):
    expert = places_ref[0] * EXP_DEV + pl.program_id(0)
    rows = rows_ref[0]
    logits = mm(rows, router_ref[...])
    logits = jnp.exp(logits - jnp.max(logits, axis=-1, keepdims=True))
    mine = lax.broadcasted_iota(jnp.int32, logits.shape, 1) == expert
    slot_gate = jnp.sum(jnp.where(mine, logits, 0.0), axis=-1, keepdims=True) / jnp.sum(
        logits, axis=-1, keepdims=True
    )
    gate_pre, up_pre = mm(rows, gate[0]), mm(rows, up[0])
    grads = grads_ref[0].astype(F32)
    pair_ref[0] = (slot_gate * grads).astype(LOW)
    sig = 1.0 / (1.0 + jnp.exp(-gate_pre))
    silu = gate_pre * sig
    act_ref[0] = (silu * up_pre).astype(LOW)
    act_grad = dot_last(pair_ref[0], down[0])
    gate_out[0] = (act_grad * up_pre * (sig + silu * (1.0 - sig))).astype(LOW)
    up_out[0] = (act_grad * silu).astype(LOW)
    pair_out = mm(act_ref[0], down[0])
    slot_ref[0] = jnp.sum(pair_out * grads, axis=-1, keepdims=True)
    weighted_ref[0] = (slot_gate * pair_out).astype(LOW)


def row_grad_body(gate_ref, up_ref, gate, up, back_ref):
    back = dot_last(gate_ref[0], gate[0]) + dot_last(up_ref[0], up[0])
    back_ref[0] = back.astype(LOW)


def expert_block(chunk, size):
    return pl.BlockSpec((1, chunk, size), lambda e, r, *p: (e, r, 0))


def expert_weight(array):
    return pl.BlockSpec((1,) + array.shape[1:], lambda e, r, *p: (e, 0, 0))


def expert_cost(experts, total, width, hidden, products):
    return pl.CostEstimate(
        flops=2 * products * experts * total * width * hidden,
        bytes_accessed=2 * experts * (4 * total * width + 3 * hidden * (total + width)),
        transcendentals=experts * total * hidden,
    )


def expert_pass(places, rows, grads, router, gate, up, down):
    experts, total, width = rows.shape
    hidden = gate.shape[-1]
    chunk = min(256, total)
    sizes = [hidden, hidden, hidden, width, width]
    return pl.pallas_call(
        expert_body,
        grid_spec=pltpu.PrefetchScalarGridSpec(
            num_scalar_prefetch=1,
            grid=(experts, total // chunk),
            in_specs=[expert_block(chunk, width)] * 2
            + [pl.BlockSpec(router.shape, lambda e, r, p: (0, 0))]
            + [expert_weight(w) for w in (gate, up, down)],
            out_specs=[expert_block(chunk, size) for size in sizes + [1]],
        ),
        out_shape=[jax.ShapeDtypeStruct((experts, total, size), LOW) for size in sizes]
        + [jax.ShapeDtypeStruct((experts, total, 1), F32)],
        compiler_params=pltpu.CompilerParams(vmem_limit_bytes=60 * 2**20),
        cost_estimate=expert_cost(experts, total, width, hidden, 4),
        name="experts",
    )(places, rows, grads, router, gate, up, down)


def row_grads(gate_grad, up_grad, gate, up):
    experts, total, hidden = gate_grad.shape
    width = gate.shape[1]
    chunk = total
    return pl.pallas_call(
        row_grad_body,
        grid=(experts, total // chunk),
        in_specs=[expert_block(chunk, hidden)] * 2 + [expert_weight(gate), expert_weight(up)],
        out_specs=expert_block(chunk, width),
        out_shape=jax.ShapeDtypeStruct((experts, total, width), LOW),
        compiler_params=pltpu.CompilerParams(vmem_limit_bytes=48 * 2**20),
        cost_estimate=expert_cost(experts, total, width, hidden, 2),
        name="row_grads",
    )(gate_grad, up_grad, gate, up)


def rope(values, cosine, sine):
    return values * cosine + pltpu.roll(values, HEAD_DIM // 2, 1) * sine


def rope_back(values, cosine, sine):
    return values * cosine - pltpu.roll(values, HEAD_DIM // 2, 1) * sine


def attend_body(
    query_raw, key_raw, value_raw, inverse, gain_query, gain_key, cosine, sine,
    segment_column, segment_row, query_ref, key_ref, value_ref, out_ref, total_ref,
):
    seq = query_raw.shape[0]
    block = min(BLOCK, seq)
    cos, sin = cosine[...], sine[...]
    query = query_raw[...] * inverse[:, 0:1] * gain_query[...]
    query_ref[...] = rope(query, cos, sin).astype(LOW)
    key = key_raw[...] * inverse[:, 1:2] * gain_key[...]
    key_ref[...] = rope(key, cos, sin).astype(LOW)
    value_ref[...] = value_raw[...].astype(LOW)
    for start in range(0, seq, block):
        stop = start + block
        at = slice(start, stop)
        scores = dot_last(query_ref[at], key_ref[:stop]) * HEAD_DIM ** (-0.5)
        row = lax.broadcasted_iota(jnp.int32, scores.shape, 0) + start
        column = lax.broadcasted_iota(jnp.int32, scores.shape, 1)
        own = segment_column[at]
        same = (own == segment_row[:, :stop]) & (own >= 0)
        scores = jnp.where((column <= row) | same, scores, -jnp.inf)
        top = jnp.max(scores, axis=-1, keepdims=True)
        probs = jnp.exp(scores - top)
        total = jnp.sum(probs, axis=-1, keepdims=True)
        probs = (probs * (1.0 / total)).astype(LOW)
        out_ref[at] = mm(probs, value_ref[:stop]).astype(LOW)
        total_ref[0, at] = top + jnp.log(total)


def attend_back_body(
    query_ref, key_ref, value_ref, grad_ref, total_ref, cosine, sine,
    segment_column, segment_row, query_out, key_out, value_out, key_sum, value_sum,
):
    seq = query_ref.shape[0]
    block = min(BLOCK, seq)
    cos, sin = cosine[...], sine[...]
    scale = HEAD_DIM ** (-0.5)
    key_sum[...] = jnp.zeros_like(key_sum)
    value_sum[...] = jnp.zeros_like(value_sum)
    for start in range(0, seq, block):
        stop = start + block
        at = slice(start, stop)
        query, grad = query_ref[at], grad_ref[at]
        scores = dot_last(key_ref[:stop], query) * scale
        row = lax.broadcasted_iota(jnp.int32, scores.shape, 0)
        column = lax.broadcasted_iota(jnp.int32, scores.shape, 1) + start
        own = segment_row[:, at]
        same = (segment_column[:stop] == own) & (own >= 0)
        allowed = (row <= column) | same
        probs = jnp.exp(jnp.where(allowed, scores - total_ref[0, :, at], -jnp.inf))
        probs_grad = dot_last(value_ref[:stop], grad)
        delta = jnp.sum(probs * probs_grad, axis=0, keepdims=True)
        score_grad = (probs * (probs_grad - delta)).astype(LOW)
        value_sum[:stop] += mm(probs.astype(LOW), grad)
        key_sum[:stop] += mm(score_grad, query)
        query_grad = (dot_first(score_grad, key_ref[:stop]) * scale).astype(LOW)
        query_out[at] = rope_back(query_grad.astype(F32), cos[at], sin[at])
    key_grad = (key_sum[...] * scale).astype(LOW)
    key_out[...] = rope_back(key_grad.astype(F32), cos, sin)
    value_out[...] = value_sum[...].astype(LOW)


def whole_block(array):
    return pl.BlockSpec(array.shape, lambda h: (0,) * array.ndim)


def head_block(rows, offset=0):
    return pl.BlockSpec((rows, HEAD_DIM), lambda h: (0, h + offset))


def attend_cost(heads, seq, products):
    return pl.CostEstimate(
        flops=products * 2 * heads * seq * seq * HEAD_DIM,
        bytes_accessed=heads * seq * HEAD_DIM * 24,
        transcendentals=heads * seq * seq,
    )


def attend(raw, inverse, gain_query, gain_key, cosine, sine, segments):
    seq = raw.shape[0]
    part = raw.shape[1] // 3
    heads = part // HEAD_DIM
    column, row = segments[:, None], segments[None, :]
    fixed = [cosine, sine, column, row]
    shape = jax.ShapeDtypeStruct((seq, part), LOW)
    return pl.pallas_call(
        attend_body,
        grid=(heads,),
        in_specs=[head_block(seq), head_block(seq, heads), head_block(seq, 2 * heads)]
        + [whole_block(inverse), head_block(1), head_block(1)]
        + [whole_block(array) for array in fixed],
        out_specs=[head_block(seq)] * 4 + [pl.BlockSpec((1, seq, 1), lambda h: (h, 0, 0))],
        out_shape=[shape] * 4 + [jax.ShapeDtypeStruct((heads, seq, 1), F32)],
        compiler_params=pltpu.CompilerParams(vmem_limit_bytes=48 * 2**20),
        cost_estimate=attend_cost(heads, seq, 2),
        name="attend",
    )(raw, raw, raw, inverse, gain_query[None], gain_key[None], *fixed)


def attend_back(query, key, value, grad, total, cosine, sine, segments):
    seq, part = query.shape
    heads = part // HEAD_DIM
    fixed = [cosine, sine, segments[:, None], segments[None, :]]

    def shape(kind):
        return jax.ShapeDtypeStruct((seq, part), kind)

    return pl.pallas_call(
        attend_back_body,
        grid=(heads,),
        in_specs=[head_block(seq)] * 4
        + [pl.BlockSpec((1, 1, seq), lambda h: (h, 0, 0))]
        + [whole_block(array) for array in fixed],
        out_specs=[head_block(seq)] * 3,
        out_shape=[shape(F32), shape(F32), shape(LOW)],
        scratch_shapes=[pltpu.VMEM((seq, HEAD_DIM), F32)] * 2,
        compiler_params=pltpu.CompilerParams(vmem_limit_bytes=48 * 2**20),
        cost_estimate=attend_cost(heads, seq, 5),
        name="attend_back",
    )(query, key, value, grad, total.reshape(heads, 1, seq), *fixed)


def tile_sum(values):
    tiles = lax.psum(values.reshape(-1, 128), "shard")
    return lax.optimization_barrier(tiles).reshape(values.shape)


def spread(block, axes, count):
    copies = jnp.broadcast_to(block[None], (count,) + block.shape)
    return lax.all_to_all(copies, axes, split_axis=0, concat_axis=0, tiled=True)


def per_device(
    inputs,
    segment_ids,
    route_ids,
    norm_gains,
    w_query,
    w_key,
    w_value,
    w_output,
    w_router,
    experts_gate,
    experts_up,
    experts_down,
    cotangent,
):
    rows = inputs[0]
    out_grad = cotangent[0]
    tokens, width = rows.shape
    capacity = tokens // 4
    ways = lax.axis_size("expert")
    shards = lax.axis_size("shard")
    both = ("expert", "shard")
    part = width // shards
    own_rows = w_query.shape[0]
    seq = tokens * shards
    my_expert = lax.axis_index("expert")
    my_shard = lax.axis_index("shard")
    devices = ways * shards
    to_slice = [(i, (i % ways) * shards + i // ways) for i in range(devices)]
    from_slice = [(b, a) for a, b in to_slice]

    three = jnp.stack([w_query, w_key, w_value], axis=1).astype(LOW)
    three = three.reshape(own_rows, 3, shards, part).transpose(2, 0, 1, 3)
    three = three.reshape(shards, own_rows, 3 * part)
    gate_low, three = tie(experts_gate.astype(LOW), three)
    grad_ring = RingGather(out_grad.astype(LOW), ways)
    grad_ring.step()
    mixed_three = jnp.zeros_like(three)
    for key in range(shards):
        other = my_shard ^ key
        piece = lax.dynamic_slice_in_dim(three, other, 1, 0)
        if key:
            piece = lax.ppermute(piece, "shard", flip_steps(shards, key))
        mixed_three = lax.dynamic_update_slice_in_dim(mixed_three, piece, other, 0)
    (experts_up, experts_down), three = tie((experts_up, experts_down), mixed_three)
    small = jnp.concatenate([norm_gains.T, w_router], axis=1).astype(LOW)
    small_all = spread(small, both, devices).reshape(width, -1)
    gains = small_all[:, :4].astype(F32).T
    weight_router = small_all[:, 4:]
    gain_attn, gain_mlp = gains[0], gains[3]
    gain_query = lax.dynamic_slice_in_dim(gains[1], my_shard * part, part)
    gain_key = lax.dynamic_slice_in_dim(gains[2], my_shard * part, part)

    my_place = jnp.array(ring_order_inverse(ways), jnp.int32)[my_expert]
    ring = jnp.array(ring_order(ways), jnp.int32)[(my_place - jnp.arange(ways)) % ways]
    slice_rows = shards * own_rows
    three_ring = RingGather(three.reshape(slice_rows, 3 * part), ways)
    inverse_rows = inverse_rms(jnp.mean(rows * rows, axis=-1, keepdims=True))
    normed = (rows * inverse_rows * gain_attn).astype(LOW)
    normed_ring = ShardGather(normed, shards)
    normed_ring.hop()
    moved_output = lax.ppermute(w_output.astype(LOW), both, to_slice)
    output_ring = RingGather(moved_output, ways)
    three_ring.step()
    three_ring.held = grad_ring.tie(three_ring.held)
    for _ in range(ways // 2 - 2):
        output_ring.step()
        three_ring.step()
        three_ring.held = output_ring.tie(three_ring.held)
    three_ring.held = normed_ring.tie(three_ring.held)
    output_ring.step()
    normed_all = normed_ring.whole(my_shard)
    weight_three = jnp.zeros((width, 3 * part), LOW)
    three_parts = three_ring.finish()
    output_parts = output_ring.finish()
    for step, piece in enumerate(three_parts):
        weight_three = lax.dynamic_update_slice_in_dim(
            weight_three, piece, ring[step] * slice_rows, 0
        )
    grad_ring.held, _ = tie(grad_ring.held, three_parts[ways // 2])
    raw = mm(normed_all, weight_three)
    query_raw, key_raw = raw[:, :part], raw[:, part : 2 * part]
    squares = jnp.stack(
        [jnp.sum(query_raw * query_raw, axis=-1), jnp.sum(key_raw * key_raw, axis=-1)]
    )
    squares = tile_sum(squares)
    inverse_qk = inverse_rms(squares / width)
    inverse_query, inverse_key = inverse_qk[0][:, None], inverse_qk[1][:, None]
    cosine, sine = rope_tables(seq)
    segments = segment_ids[0]
    query, key, value, attended, log_total = attend(
        raw, inverse_qk.T, gain_query, gain_key, cosine, sine, segments
    )
    grad_ring.step()
    attended = grad_ring.tie(attended)
    grad_ring.step()
    weight_output = jnp.zeros((own_rows * ways, width), LOW)
    for step, piece in enumerate(output_parts):
        weight_output = lax.dynamic_update_slice_in_dim(
            weight_output, piece, ring[step] * own_rows, 0
        )
    projected = mm(attended, weight_output).astype(LOW)
    projected = ShardScatter(shard_pieces(projected, shards, my_shard), shards)
    projected.hop()
    grad_ring.step()
    hidden = rows + projected.finish()
    inverse_hidden = inverse_rms(jnp.mean(hidden * hidden, axis=-1, keepdims=True))
    mlp_in = (hidden * inverse_hidden * gain_mlp).astype(LOW)

    routes_all = jnp.take(spread(route_ids[0].T, "expert", ways), ring, axis=0)
    mlp_in = grad_ring.tie(mlp_in)
    mlp_ring = RingGather(mlp_in, ways)
    mlp_ring.step()
    expert_names = my_expert * EXP_DEV + jnp.arange(EXP_DEV, dtype=jnp.int32)
    chosen = jnp.any(routes_all[None] == expert_names[:, None, None, None], axis=2)
    places = jnp.arange(tokens, dtype=jnp.int32)
    before = (places[:, None] < places[None, :]).astype(LOW)
    rank = jnp.einsum("lbt,tu->lbu", chosen.astype(LOW), before, preferred_element_type=F32)
    rank = jnp.where(chosen, rank.astype(jnp.int32), -1)
    slots = jnp.arange(capacity, dtype=jnp.int32)
    pick = rank[:, :, None, :] == slots[None, None, :, None]
    pick_low = pick.astype(LOW)

    weights_gate = lax.all_gather(gate_low, "shard", axis=1, tiled=True)
    weights_up = lax.all_gather(experts_up.astype(LOW), "shard", axis=1, tiled=True)
    weights_down = lax.all_gather(experts_down.astype(LOW), "shard", axis=1, tiled=True)

    logits = mm(mlp_in, weight_router)
    router = jax.nn.softmax(logits, axis=-1)

    def combine(values):
        return jnp.einsum(
            "lbct,lbcd->btd",
            pick_low,
            values.reshape(EXP_DEV, ways, capacity, width),
            preferred_element_type=F32,
        ).astype(LOW)

    expert_grads = dispatch(pick_low, grad_ring.finish())
    expert_rows = dispatch(pick_low, mlp_ring.finish())
    activation, gate_pre_grad, up_pre_grad, pair_grads, weighted, slot_grad = expert_pass(
        jnp.stack([my_expert, my_shard]).astype(jnp.int32),
        expert_rows,
        expert_grads,
        weight_router,
        weights_gate,
        weights_up,
        weights_down,
    )

    def weight_grad(spec, left, right):
        return jnp.einsum(spec, left, right, preferred_element_type=F32).astype(LOW)

    def expert_sum(grad):
        return lax.psum_scatter(grad, "shard", scatter_dimension=1, tiled=True)

    def weight_grad_sum(spec, left, right):
        return expert_sum(weight_grad(spec, left, right))

    grad_down = weight_grad("erf,erd->efd", activation, pair_grads)
    (back_gate, back_up), grad_down = tie((gate_pre_grad, up_pre_grad), grad_down)
    grad_down = expert_sum(grad_down)
    weighted, _ = tie(weighted, back_up)
    mixed_sum = combine(weighted)
    mixed_ring = RingScatter(lambda j: mixed_sum[j], ways)
    mixed_ring.step()
    rows_sum = mixed_ring.tie(combine(row_grads(back_gate, back_up, weights_gate, weights_up)))
    rows_ring = RingScatter(lambda j: rows_sum[j], ways)
    rows_ring.step()
    gate_pre_grad = rows_ring.tie(gate_pre_grad)
    grad_gate = weight_grad_sum("erd,erf->edf", expert_rows, gate_pre_grad)
    rows_ring.step()
    slot_grad = rows_ring.tie(slot_grad)
    slot_grad = slot_grad.reshape(EXP_DEV, ways, capacity, 1)
    token_grad = jnp.sum(jnp.where(pick, slot_grad, 0.0), axis=2).transpose(1, 0, 2)
    back_order = (my_place - jnp.array(ring_order_inverse(ways), jnp.int32)) % ways
    token_grad = jnp.take(token_grad, back_order, axis=0)
    router_grad = lax.all_to_all(token_grad, "expert", split_axis=0, concat_axis=0, tiled=True)
    router_grad = router_grad.reshape(ways * EXP_DEV, tokens).T
    rows_ring.step()
    router_grad = rows_ring.tie(router_grad)
    mlp_grad = rows_ring.finish()
    logit_grad = (
        router * (router_grad - jnp.sum(router * router_grad, axis=-1, keepdims=True))
    ).astype(LOW)
    grad_router = dot_first(mlp_in, logit_grad)
    mlp_in_grad = mlp_grad + dot_last(logit_grad, weight_router)
    hidden_part, gain_mlp_grad = rms_back(hidden, inverse_hidden, gain_mlp, mlp_in_grad)
    hidden_grad = out_grad + hidden_part
    hidden_low = hidden_grad.astype(LOW)
    mixed_ring.state, hidden_low = tie(mixed_ring.state, hidden_low)
    attn_ring = ShardGather(hidden_low, shards)
    attn_ring.hop()
    mixed_ring.step()
    attn_ring.held = mixed_ring.tie(attn_ring.held)
    mixed_ring.step()
    up_pre_grad, _ = tie(up_pre_grad, attn_ring.held)
    grad_up = weight_grad_sum("erd,erf->edf", expert_rows, up_pre_grad)
    attn_grad = attn_ring.whole(my_shard)
    grad_output = dot_first(attended, attn_grad).astype(LOW).reshape(width, part)

    def piece_of(whole):
        size = whole.shape[0] // ways
        return lambda j: lax.dynamic_slice_in_dim(whole, ring[j] * size, size, 0)

    attended_grad = dot_last(attn_grad, weight_output).astype(LOW)

    query_grad, key_grad, value_grad = attend_back(
        query, key, value, attended_grad, log_total, cosine, sine, segments
    )
    query_grad = mixed_ring.tie(query_grad)
    mixed_ring.step()
    inner = jnp.stack(
        [
            jnp.sum(query_raw * gain_query * query_grad, axis=-1),
            jnp.sum(key_raw * gain_key * key_grad, axis=-1),
        ]
    )
    inner, grad_down = tie(inner, grad_down)
    grad_down = grad_down.astype(F32)
    inner = tile_sum(inner) / width
    gain_query_grad = jnp.sum(query_grad * query_raw * inverse_query, axis=0)
    gain_key_grad = jnp.sum(key_grad * key_raw * inverse_key, axis=0)
    query_raw_grad = inverse_query * gain_query * query_grad - query_raw * (
        inverse_query**3 * inner[0][:, None]
    )
    key_raw_grad = inverse_key * gain_key * key_grad - key_raw * (
        inverse_key**3 * inner[1][:, None]
    )
    three_grad = jnp.concatenate(
        [query_raw_grad.astype(LOW), key_raw_grad.astype(LOW), value_grad], axis=1
    )
    normed_grad = dot_last(three_grad, weight_three).astype(LOW)
    normed_sum = ShardScatter(shard_pieces(normed_grad, shards, my_shard), shards)
    while 2 * normed_sum.distance < shards:
        normed_sum.hop()
    grad_three = dot_first(normed_all, three_grad).astype(LOW)

    grad_three = mixed_ring.tie(grad_three)
    output = hidden + mixed_ring.finish()
    three_piece, output_piece = piece_of(grad_three), piece_of(grad_output)
    three_ring = RingScatter(
        lambda j: jnp.concatenate([three_piece(j), output_piece(j)], axis=1), ways
    )
    for step in range(ways // 2):
        three_ring.step()
        if step == ways // 2 - 2:
            three_ring.state, grad_gate = tie(three_ring.state, grad_gate)
            grad_gate = grad_gate.astype(F32)
            normed_sum.hop(three_ring.state)
    rows_part, gain_attn_grad = rms_back(rows, inverse_rows, gain_attn, normed_sum.finish())
    input_grad = hidden_grad + rows_part
    joined = three_ring.finish().astype(LOW)
    grad_three = joined[:, : 3 * part]
    grad_output = joined[:, 3 * part :].reshape(own_rows, width)
    grad_output = lax.ppermute(grad_output, both, from_slice).astype(F32)
    grad_up, _ = tie(grad_up, grad_three)
    grad_up = grad_up.astype(F32)
    grad_three = lax.all_to_all(
        grad_three.reshape(shards, own_rows, 3 * part),
        "shard",
        split_axis=0,
        concat_axis=0,
        tiled=True,
    )
    grad_three = grad_three.reshape(shards, own_rows, 3, part).transpose(2, 1, 0, 3)
    grad_three = grad_three.reshape(3, own_rows, width).astype(F32)

    zeros = jnp.zeros((width,), F32)

    def placed(piece):
        return lax.dynamic_update_slice_in_dim(zeros, piece, my_shard * part, 0)

    gain_grads = jnp.stack(
        [gain_attn_grad, placed(gain_query_grad), placed(gain_key_grad), gain_mlp_grad], axis=1
    )
    small_grad = jnp.concatenate([gain_grads, grad_router], axis=1)
    small_grad = lax.all_to_all(
        small_grad.reshape(devices, own_rows, -1), both, split_axis=0, concat_axis=0, tiled=True
    )
    small_grad = jnp.sum(small_grad, axis=0)
    return (
        output[None],
        input_grad[None],
        small_grad[:, :4].T,
        grad_three[0],
        grad_three[1],
        grad_three[2],
        grad_output,
        small_grad[:, 4:],
        grad_gate,
        grad_up,
        grad_down,
    )


def solution(mesh):
    tokens = P("expert", "shard", None)
    flat = P(("expert", "shard"), None)
    return jax.shard_map(
        per_device,
        mesh=mesh,
        in_specs=(
            tokens,
            P("expert", None),
            tokens,
            P(None, ("expert", "shard")),
            flat,
            flat,
            flat,
            flat,
            flat,
            tokens,
            tokens,
            tokens,
            tokens,
        ),
        out_specs=(
            tokens,
            tokens,
            P(None, ("expert", "shard")),
            flat,
            flat,
            flat,
            flat,
            flat,
            tokens,
            tokens,
            tokens,
        ),
        check_vma=False,
    )
```

time: 2870 us -> 965 us (0.34)
  waiting for transfers between devices: 2150 us -> 352 us
  matrix products: 294 us -> 105 us
  Pallas kernels: 0 us -> 129 us
  local copies, waits for them, and re-layouts: 172 us -> 85.3 us
  starting transfers between devices: 24.7 us -> 98.2 us
  blocking collectives: 70.1 us -> 33.2 us
    reduce_scatter x9 -> x3, waiting for transfers between devices: 1180 us -> 0.01 us  [expert_sum(): return lax.psum_scatter(grad, 'shard', scatter_dimension=1, tiled=True)]
    all_to_all x4, waiting for transfers between devices: 608 us -> 7.09 us  [the longest x1 6.26 us: per_device(): lax.all_to_all(small_grad.reshape(devices, own_rows, -1), both, split_axi...]
    ppermute x0 -> x66, waiting for transfers between devices: none -> 344 us  [the longest x16 115 us: step(): held[step] = lax.ppermute(held[step - 1], 'expert', self.forward)]
    all_gather x9 -> x3, waiting for transfers between devices: 219 us -> 1.09 us  [the longest x1 1.07 us: per_device(): lax.all_gather(experts_down.astype(LOW), 'shard', axis=1, tiled=True)]
    dot_general x29 -> x15, matrix products: 292 us -> 105 us  [the longest x3 48.2 us: weight_grad(): return jnp.einsum(spec, left, right, preferred_element_type=F32).astype(LOW)]
    unnamed x22 -> x6, waiting for transfers between devices: 142 us -> 0.1 us
    pallas_call x0 -> x6, Pallas kernels: none -> 129 us  [the longest x1 54.2 us: expert_pass(): pl.pallas_call(expert_body, grid_spec=pltpu.PrefetchScalarGridSpec(num_sc...]
    ppermute x0 -> x66, starting transfers between devices: none -> 77.2 us  [the longest x16 16.1 us: step(): held[step] = lax.ppermute(held[step - 1], 'expert', self.forward)]
  transfers between devices with their start and end apart: 24 -> 76, of which waited for: 19 -> 29; matrix products, arithmetic and copies ran while one was open for 16% -> 27% of each run, Pallas kernels for 0% -> 8%
where the time goes in v1:
time: 965 us; the launch traced here: 947 us
  waiting for transfers between devices  352 us (36%)
  Pallas kernels  129 us (13%)
  other arithmetic  118 us (12%)
  matrix products  105 us (11%)
  starting transfers between devices  98.2 us (10%)
  local copies, waits for them, and re-layouts  85.3 us (9%)
  blocking collectives  33.2 us (3%)
  between operations  26.4 us (3%)
    ppermute x16, waiting for transfers between devices, step(): held[step] = lax.ppermute(held[step - 1], 'expert', self.forward)  115 us
    ppermute x12, waiting for transfers between devices, step(): right = lax.ppermute(right, 'expert', self.forward)  98.8 us
    pallas_call x1, Pallas kernels, expert_pass(): pl.pallas_call(expert_body, grid_spec=pltpu.PrefetchScalarGridSpec(num_sc...  54.2 us
    ppermute x6, waiting for transfers between devices, hop(): got = lax.ppermute(self.held.pop(key), 'shard', steps)  51.1 us
    dot_general x3, matrix products, weight_grad(): return jnp.einsum(spec, left, right, preferred_element_type=F32).astype(LOW)  48.2 us
    convert_element_type x11, other arithmetic, add(): return (got.astype(F32) + self.piece(index).astype(F32)).astype(LOW)  28.2 us
    pallas_call x1, Pallas kernels, row_grads(): pl.pallas_call(row_grad_body, grid=(experts, total // chunk), in_specs=[e...  27.7 us
    ppermute x1, waiting for transfers between devices, per_device(): moved_output = lax.ppermute(w_output.astype(LOW), both, to_slice)  27.2 us
  transfers between devices with their start and end apart: 76, of which 29 were waited for; matrix products, arithmetic and copies ran while one was open for 27% of the time, Pallas kernels for 8%

profile of v1, /device:TPU:9, one launch (start us, length us, event | category | flops | bytes accessed | tf_op | source)
XLA Modules:
  0.0 946.9 jit_solution(15234686607428679913)
XLA Ops:
  33.2 7.6 convert_element_type.366
  63.4 27.2 %collective-permute-done.9 = bf16[64,2048]{1,0:T(8,128)(2,1)} collective-permute-done((bf16[64,2048]{1,0:T(8,128)(2,1)}, bf16[64,2048]{1,0:T(8,128)(2,1)}, u32[]{:S(2)}, u32[]{:S(2)}) %collective-permute-start.9) | collective-permute-done | bytes 262176 | tf_op jit(solution)/shard_map/ppermute | solution.py:519
  99.2 9.2 collective-permute-done.4
  115.5 10.6 %collective-permute-done.7 = bf16[256,1536]{1,0:T(8,128)(2,1)} collective-permute-done((bf16[256,1536]{1,0:T(8,128)(2,1)}, bf16[256,1536]{1,0:T(8,128)(2,1)}, u32[]{:S(2)}, u32[]{:S(2)}) %collective-permute-start.7) | collective-permute-done | bytes 786464 | tf_op jit(solution)/shard_map/ppermute | solution.py:86
  172.2 12.5 %collective-permute-done.23 = bf16[64,2048]{1,0:T(8,128)(2,1)S(1)} collective-permute-done((bf16[64,2048]{1,0:T(8,128)(2,1)S(1)}, bf16[64,2048]{1,0:T(8,128)(2,1)S(1)}, u32[]{:S(2)}, u32[]{:S(2)}) %collective-permute-start.23) | collective-permute-done | bytes 262176 | tf_op jit(solution)/shard_map/ppermute | solution.py:86
  201.1 9.1 psum.14
  211.1 16.2 %attend.1 = (bf16[1024,512]{1,0:T(8,128)(2,1)S(1)}, bf16[1024,512]{1,0:T(8,128)(2,1)S(1)}, bf16[1024,512]{1,0:T(8,128)(2,1)S(1)}, bf16[1024,512]{1,0:T(8,128)(2,1)}, f32[4,1024,1]{2,1,0:T(8,128)}) custom-call(f32[1024,1536]{1,0:T(8,128)} %copy-done.19, f32[1024,1536]{1,0:T(8,128)} %copy-done.19, f32[1024,1536]{1,0:T(8,128)} %copy-done.19, ...), custom_call_target="tpu_custom_call" | custom-call | flops 2147483648 | bytes 12582912 | tf_op jit(solution)/shard_map/attend/pallas_call | solution.py:411
  237.4 20.0 %collective-permute-done.28.refs_4_ = bf16[256,2048]{1,0:T(8,128)(2,1)S(1)} collective-permute-done((bf16[256,2048]{1,0:T(8,128)(2,1)}, bf16[256,2048]{1,0:T(8,128)(2,1)S(1)}, u32[]{:S(2)}, u32[]{:S(2)}) %collective-permute-start.28) | collective-permute-done | bytes 1048608 | tf_op jit(solution)/shard_map/ppermute | solution.py:86
  259.3 17.0 %collective-permute-done.27 = bf16[256,2048]{1,0:T(8,128)(2,1)S(1)} collective-permute-done((bf16[256,2048]{1,0:T(8,128)(2,1)S(1)}, bf16[256,2048]{1,0:T(8,128)(2,1)S(1)}, u32[]{:S(2)}, u32[]{:S(2)}) %collective-permute-start.27) | collective-permute-done | bytes 1048608 | tf_op jit(solution)/shard_map/ppermute | solution.py:180
  283.1 20.7 %collective-permute-done.31.refs_2_ = bf16[256,2048]{1,0:T(8,128)(2,1)S(1)} collective-permute-done((bf16[256,2048]{1,0:T(8,128)(2,1)S(1)}, bf16[256,2048]{1,0:T(8,128)(2,1)S(1)}, u32[]{:S(2)}, u32[]{:S(2)}) %collective-permute-start.31) | collective-permute-done | bytes 1048608 | tf_op jit(solution)/shard_map/ppermute | solution.py:86
  307.1 18.9 %collective-permute-done.32.refs_3_ = bf16[256,2048]{1,0:T(8,128)(2,1)} collective-permute-done((bf16[256,2048]{1,0:T(8,128)(2,1)S(1)}, bf16[256,2048]{1,0:T(8,128)(2,1)}, u32[]{:S(2)}, u32[]{:S(2)}) %collective-permute-start.32) | collective-permute-done | bytes 1048608 | tf_op jit(solution)/shard_map/ppermute | solution.py:86
  333.0 14.9 %collective-permute-done.33.refs_4_ = bf16[256,2048]{1,0:T(8,128)(2,1)} collective-permute-done((bf16[256,2048]{1,0:T(8,128)(2,1)}, bf16[256,2048]{1,0:T(8,128)(2,1)}, u32[]{:S(2)}, u32[]{:S(2)}) %collective-permute-start.33) | collective-permute-done | bytes 1048608 | tf_op jit(solution)/shard_map/ppermute | solution.py:86
  353.7 7.6 dispatch.3.grads_ref
  361.3 9.4 collective-permute-done.34.refs_5_
  379.4 54.2 %experts.1 = (bf16[4,512,1024]{2,1,0:T(8,128)(2,1)}, bf16[4,512,1024]{2,1,0:T(8,128)(2,1)}, bf16[4,512,1024]{2,1,0:T(8,128)(2,1)}, bf16[4,512,2048]{2,1,0:T(8,12...) custom-call(s32[2]{0:T(128)} %pad_add_fusion.places_ref, bf16[4,512,2048]{2,1,0:T(8,128)(2,1)} %dispatch.2.rows_ref, ...), custom_call_target="tpu_custom_call" | custom-call | flops 34359738368 | bytes 96468992 | tf_op jit(solution)/shard_map/experts/pallas_call | solution.py:284
  433.6 16.4 %convolution_convert_fusion.2 = bf16[4,1024,2048]{2,1,0:T(8,128)(2,1)} fusion(bf16[4,512,1024]{2,1,0:T(8,128)(2,1)} %get-tuple-element.182, bf16[4,512,2048]{2,1,0:T(8,128)(2,1)} %get-tuple-element.183), kind=kOutput, calls=%fused_computation.7 | convolution fusion | flops 8598323200 | bytes 29360128 | tf_op jit(solution)/shard_map/erf,erd->efd/dot_general | solution.py:609
  461.4 27.7 %row_grads.1 = bf16[4,512,2048]{2,1,0:T(8,128)(2,1)} custom-call(bf16[4,512,1024]{2,1,0:T(8,128)(2,1)S(1)} %copy-done.15, bf16[4,512,1024]{2,1,0:T(8,128)(2,1)} %get-tuple-element.226.up_ref, bf16[4,2048,1024]{2,1,0:T(8,128)(2,1)} %all-gather.4.cloned.1.call-done.gate, bf16[4,2048,1024]{2,1,0:T(8,128)(2,1)} %all-gather.6.cloned.1.call-done.up), custom_call_target="tpu_custom_call" | custom-call | flops 17179869184 | bytes 96468992 | tf_op jit(solution)/shard_map/row_grads/pallas_call | solution.py:306
  489.2 9.1 bitcast_convert_fusion
  504.0 20.0 %collective-permute-done.39 = bf16[256,2048]{1,0:T(8,128)(2,1)S(1)} collective-permute-done((bf16[256,2048]{1,0:T(8,128)(2,1)S(1)}, bf16[256,2048]{1,0:T(8,128)(2,1)S(1)}, u32[]{:S(2)}, u32[]{:S(2)}) %collective-permute-start.39) | collective-permute-done | bytes 1048608 | tf_op jit(solution)/shard_map/ppermute | solution.py:123
  526.6 15.9 %convolution_convert_fusion.1 = bf16[4,2048,1024]{2,1,0:T(8,128)(2,1)} fusion(bf16[4,512,2048]{2,1,0:T(8,128)(2,1)} %dispatch.2.rows_ref, bf16[4,512,1024]{2,1,0:T(8,128)(2,1)} %get-tuple-element.221.gate_ref), kind=kOutput, calls=%fused_computation.6 | convolution fusion | flops 8598323200 | bytes 29360128 | tf_op jit(solution)/shard_map/erd,erf->edf/dot_general | solution.py:609
  544.0 19.2 %collective-permute-done.40 = bf16[256,2048]{1,0:T(8,128)(2,1)S(1)} collective-permute-done((bf16[256,2048]{1,0:T(8,128)(2,1)}, bf16[256,2048]{1,0:T(8,128)(2,1)S(1)}, u32[]{:S(2)}, u32[]{:S(2)}) %collective-permute-start.40) | collective-permute-done | bytes 1048608 | tf_op jit(solution)/shard_map/ppermute | solution.py:123
  572.5 17.4 %all_to_all.25 = f32[8,4,256]{2,1,0:T(4,128)S(1)} all-to-all(f32[8,4,256]{2,1,0:T(4,128)S(1)} %broadcast_select_fusion.1), channel_id=1, replica_groups=mesh['expert'=8,'shard'=4] {'expert'}, dimensions={0} | all-to-all | bytes 65536 | tf_op jit(solution)/shard_map/all_to_all | solution.py:635
  595.9 15.2 %collective-permute-done.44 = bf16[256,2048]{1,0:T(8,128)(2,1)S(1)} collective-permute-done((bf16[256,2048]{1,0:T(8,128)(2,1)S(1)}, bf16[256,2048]{1,0:T(8,128)(2,1)S(1)}, u32[]{:S(2)}, u32[]{:S(2)}) %collective-permute-start.44) | collective-permute-done | bytes 1048608 | tf_op jit(solution)/shard_map/ppermute | solution.py:123
  617.9 15.3 %collective-permute-done.47 = bf16[256,2048]{1,0:T(8,128)(2,1)S(1)} collective-permute-done((bf16[256,2048]{1,0:T(8,128)(2,1)S(1)}, bf16[256,2048]{1,0:T(8,128)(2,1)S(1)}, u32[]{:S(2)}, u32[]{:S(2)}) %collective-permute-start.47) | collective-permute-done | bytes 1048608 | tf_op jit(solution)/shard_map/ppermute | solution.py:123
  636.8 26.1 %collective-permute-done.46 = bf16[256,2048]{1,0:T(8,128)(2,1)} collective-permute-done((bf16[256,2048]{1,0:T(8,128)(2,1)}, bf16[256,2048]{1,0:T(8,128)(2,1)}, u32[]{:S(2)}, u32[]{:S(2)}) %collective-permute-start.46) | collective-permute-done | bytes 1048608 | tf_op jit(solution)/shard_map/ppermute | solution.py:152
  662.9 15.9 %convolution_convert_fusion = bf16[4,2048,1024]{2,1,0:T(8,128)(2,1)} fusion(bf16[4,512,2048]{2,1,0:T(8,128)(2,1)} %dispatch.2.rows_ref, bf16[4,512,1024]{2,1,0:T(8,128)(2,1)} %get-tuple-element.226.up_ref), kind=kOutput, calls=%fused_computation.5 | convolution fusion | flops 8598323200 | bytes 29360128 | tf_op jit(solution)/shard_map/erd,erf->edf/dot_general | solution.py:609
  678.9 9.2 collective-permute-start.49
  715.3 15.3 %attend_back.1 = (f32[1024,512]{1,0:T(8,128)}, f32[1024,512]{1,0:T(8,128)}, bf16[1024,512]{1,0:T(8,128)(2,1)S(1)}) custom-call(bf16[1024,512]{1,0:T(8,128)(2,1)S(1)} %copy-done.10, bf16[1024,512]{1,0:T(8,128)(2,1)S(1)} %copy-done.12, bf16[1024,512]{1,0:T(8,128)(2,1)S(1)} %copy-done.14, bf16[1024,512]{1,0:T(8,128)(2,1)} %convolution_convert_fusion.7.grad_ref, ...), custom_call_target="tpu_custom_call" | custom-call | flops 5368709120 | bytes 12582912 | tf_op jit(solution)/shard_map/attend_back/pallas_call | solution.py:433
  755.5 7.8 convolution_convert_fusion.3
  773.3 17.6 %collective-permute-done.58 = bf16[256,2048]{1,0:T(8,128)(2,1)} collective-permute-done((bf16[256,2048]{1,0:T(8,128)(2,1)}, bf16[256,2048]{1,0:T(8,128)(2,1)}, u32[]{:S(2)}, u32[]{:S(2)}) %collective-permute-start.58) | collective-permute-done | bytes 1048608 | tf_op jit(solution)/shard_map/ppermute | solution.py:123
  793.2 8.8 convolution_convert_fusion.4
  847.0 32.9 %collective-permute-done.57 = bf16[256,2048]{1,0:T(8,128)(2,1)S(1)} collective-permute-done((bf16[256,2048]{1,0:T(8,128)(2,1)}, bf16[256,2048]{1,0:T(8,128)(2,1)S(1)}, u32[]{:S(2)}, u32[]{:S(2)}) %collective-permute-start.57) | collective-permute-done | bytes 1048608 | tf_op jit(solution)/shard_map/ppermute | solution.py:180
  (492 shorter events, 375.2 us)
Async XLA Ops:
  7.2 371.1 %all-gather.4.cloned.1.call-start = ((), (), s32[]{:S(2)}) async-start(), calls=%async_computation.8 | async-start | bytes 20971520 | tf_op jit(solution)/shard_map/all_gather | solution.py:581
  19.3 359.0 %all-gather.6.cloned.1.call-start = ((), (), s32[]{:S(2)}) async-start(), calls=%async_computation.9 | async-start | bytes 20971520 | tf_op jit(solution)/shard_map/all_gather | solution.py:582
  40.9 338.6 %all-gather.8.cloned.1.call-start = ((), (), s32[]{:S(2)}) async-start(), calls=%async_computation.10 | async-start | bytes 20971520 | tf_op jit(solution)/shard_map/all_gather | solution.py:583
  48.9 59.5 %collective-permute-start.5 = (bf16[256,2048]{1,0:T(8,128)(2,1)S(1)}, bf16[256,2048]{1,0:T(8,128)(2,1)}, u32[]{:S(2)}, u32[]{:S(2)}) collective-permute-start(bf16[256,2048]{1,0:T(8,128)(2,1)S(1)} %bitcast_convert_fusion.2.refs_1_), channel_id=1, source_target_pairs={{0,8},{8,16},{16,24},{24,28},{28,20},{20,12},{12,4},{4,0},{1,9},{9... | collective-permute-start | bytes 3145736 | tf_op jit(solution)/shard_map/ppermute | solution.py:86
  50.2 58.2 %collective-permute-start.6 = (bf16[256,2048]{1,0:T(8,128)(2,1)S(1)}, bf16[256,2048]{1,0:T(8,128)(2,1)}, u32[]{:S(2)}, u32[]{:S(2)}) collective-permute-start(bf16[256,2048]{1,0:T(8,128)(2,1)S(1)} %bitcast_convert_fusion.2.refs_1_), channel_id=1, source_target_pairs={{8,0},{16,8},{24,16},{28,24},{20,28},{12,20},{4,12},{0,4},{9,1},{1... | collective-permute-start | bytes 3145736 | tf_op jit(solution)/shard_map/ppermute | solution.py:89
  51.1 39.5 %collective-permute-start.9 = (bf16[64,2048]{1,0:T(8,128)(2,1)}, bf16[64,2048]{1,0:T(8,128)(2,1)}, u32[]{:S(2)}, u32[]{:S(2)}) collective-permute-start(bf16[64,2048]{1,0:T(8,128)(2,1)} %convert_element_type.352), channel_id=1, source_target_pairs={{0,0},{1,4},{2,8},{3,12},{4,16},{5,20},{6,24},{7,28},{8,1},{9,5},{... | collective-permute-start | bytes 786440 | tf_op jit(solution)/shard_map/ppermute | solution.py:519
  55.1 36.3 %all-to-all-start = ((bf16[32,2,1152]{2,1,0:T(2,128)(2,1)}), bf16[32,2,1152]{2,1,0:T(2,128)(2,1)}, u32[]{:S(2)}, u32[]{:S(2)}) async-start(bf16[32,2,1152]{2,1,0:T(2,128)(2,1)} %reshape.434), calls=%async_computation | async-start | bytes 294912 | tf_op jit(solution)/shard_map/all_to_all | solution.py:455
  61.6 33.2 %collective-permute-start.3 = (bf16[256,1536]{1,0:T(8,128)(2,1)}, bf16[256,1536]{1,0:T(8,128)(2,1)}, u32[]{:S(2)}, u32[]{:S(2)}) collective-permute-start(bf16[256,1536]{1,0:T(8,128)(2,1)} %bitcast.2), channel_id=1, source_target_pairs={{0,8},{8,16},{16,24},{24,28},{28,20},{20,12},{12,4},{4,0},{1,9},{9... | collective-permute-start | bytes 2359304 | tf_op jit(solution)/shard_map/ppermute | solution.py:86
  62.9 45.6 %collective-permute-start.4 = (bf16[256,1536]{1,0:T(8,128)(2,1)}, bf16[256,1536]{1,0:T(8,128)(2,1)}, u32[]{:S(2)}, u32[]{:S(2)}) collective-permute-start(bf16[256,1536]{1,0:T(8,128)(2,1)} %bitcast.2), channel_id=1, source_target_pairs={{8,0},{16,8},{24,16},{28,24},{20,28},{12,20},{4,12},{0,4},{9,1},{1... | collective-permute-start | bytes 2359304 | tf_op jit(solution)/shard_map/ppermute | solution.py:89
  114.1 43.3 %collective-permute-start.16 = (bf16[256,2048]{1,0:T(8,128)(2,1)}, bf16[256,2048]{1,0:T(8,128)(2,1)}, u32[]{:S(2)}, u32[]{:S(2)}) collective-permute-start(bf16[256,2048]{1,0:T(8,128)(2,1)} %fusion.17), channel_id=1, source_target_pairs={{0,2},{1,3},{2,0},{3,1},{4,6},{5,7},{6,4},{7,5},{8,10},{9,11},{10,... | collective-permute-start | bytes 3145736 | tf_op jit(solution)/shard_map/ppermute | solution.py:152
  155.9 28.9 %collective-permute-start.24 = (bf16[64,2048]{1,0:T(8,128)(2,1)}, bf16[64,2048]{1,0:T(8,128)(2,1)S(1)}, u32[]{:S(2)}, u32[]{:S(2)}) collective-permute-start(bf16[64,2048]{1,0:T(8,128)(2,1)} %collective-permute-done.15), channel_id=1, source_target_pairs={{8,0},{16,8},{24,16},{28,24},{20,28},{12,20},{4,12},{0,4},{9,1},{1... | collective-permute-start | bytes 786440 | tf_op jit(solution)/shard_map/ppermute | solution.py:89
  157.4 28.4 %collective-permute-start.19 = (bf16[256,1536]{1,0:T(8,128)(2,1)}, bf16[256,1536]{1,0:T(8,128)(2,1)S(1)}, u32[]{:S(2)}, u32[]{:S(2)}) collective-permute-start(bf16[256,1536]{1,0:T(8,128)(2,1)} %collective-permute-done.12), channel_id=1, source_target_pairs={{0,8},{8,16},{16,24},{24,28},{28,20},{20,12},{12,4},{4,0},{1,9},{9... | collective-permute-start | bytes 2359304 | tf_op jit(solution)/shard_map/ppermute | solution.py:86
  157.4 33.6 %collective-permute-start.17 = (bf16[256,2048]{1,0:T(8,128)(2,1)}, bf16[256,2048]{1,0:T(8,128)(2,1)S(1)}, u32[]{:S(2)}, u32[]{:S(2)}) collective-permute-start(bf16[256,2048]{1,0:T(8,128)(2,1)} %fusion.17), channel_id=1, source_target_pairs={{0,1},{1,0},{2,3},{3,2},{4,5},{5,4},{6,7},{7,6},{8,9},{9,8},{10,11... | collective-permute-start | bytes 3145736 | tf_op jit(solution)/shard_map/ppermute | solution.py:152
  159.7 31.5 %collective-permute-start.18 = (bf16[256,2048]{1,0:T(8,128)(2,1)}, bf16[256,2048]{1,0:T(8,128)(2,1)S(1)}, u32[]{:S(2)}, u32[]{:S(2)}) collective-permute-start(bf16[256,2048]{1,0:T(8,128)(2,1)} %collective-permute-done.16), channel_id=1, source_target_pairs={{0,1},{1,0},{2,3},{3,2},{4,5},{5,4},{6,7},{7,6},{8,9},{9,8},{10,11... | collective-permute-start | bytes 3145736 | tf_op jit(solution)/shard_map/ppermute | solution.py:152
  185.8 41.5 %collective-permute-start.20 = (bf16[256,2048]{1,0:T(8,128)(2,1)}, bf16[256,2048]{1,0:T(8,128)(2,1)}, u32[]{:S(2)}, u32[]{:S(2)}) collective-permute-start(bf16[256,2048]{1,0:T(8,128)(2,1)} %collective-permute-done.5.refs_2_), channel_id=1, source_target_pairs={{0,8},{8,16},{16,24},{24,28},{28,20},{20,12},{12,4},{4,0},{1,9},{9... | collective-permute-start | bytes 3145736 | tf_op jit(solution)/shard_map/ppermute | solution.py:86
  186.2 41.1 %collective-permute-start.21 = (bf16[256,2048]{1,0:T(8,128)(2,1)}, bf16[256,2048]{1,0:T(8,128)(2,1)}, u32[]{:S(2)}, u32[]{:S(2)}) collective-permute-start(bf16[256,2048]{1,0:T(8,128)(2,1)} %collective-permute-done.6.refs_8_), channel_id=1, source_target_pairs={{8,0},{16,8},{24,16},{28,24},{20,28},{12,20},{4,12},{0,4},{9,1},{1... | collective-permute-start | bytes 3145736 | tf_op jit(solution)/shard_map/ppermute | solution.py:89
  235.9 40.4 %collective-permute-start.27 = (bf16[256,2048]{1,0:T(8,128)(2,1)S(1)}, bf16[256,2048]{1,0:T(8,128)(2,1)S(1)}, u32[]{:S(2)}, u32[]{:S(2)}) collective-permute-start(bf16[256,2048]{1,0:T(8,128)(2,1)S(1)} %add_convert_fusion.8), channel_id=1, source_target_pairs={{0,2},{1,3},{2,0},{3,1},{4,6},{5,7},{6,4},{7,5},{8,10},{9,11},{10,... | collective-permute-start | bytes 3145736 | tf_op jit(solution)/shard_map/ppermute | solution.py:180
  237.4 39.9 %collective-permute-start.30 = (bf16[256,2048]{1,0:T(8,128)(2,1)}, bf16[256,2048]{1,0:T(8,128)(2,1)S(1)}, u32[]{:S(2)}, u32[]{:S(2)}) collective-permute-start(bf16[256,2048]{1,0:T(8,128)(2,1)} %collective-permute-done.21.refs_7_), channel_id=1, source_target_pairs={{8,0},{16,8},{24,16},{28,24},{20,28},{12,20},{4,12},{0,4},{9,1},{1... | collective-permute-start | bytes 3145736 | tf_op jit(solution)/shard_map/ppermute | solution.py:89
  332.8 407.1 %reduce-scatter.4.cloned.1.call-start = ((), (), s32[]{:S(2)}) async-start(), calls=%async_computation.11 | async-start | bytes 20971520 | tf_op jit(solution)/shard_map/reduce_scatter | solution.py:612
  332.9 28.4 %collective-permute-start.37 = (bf16[256,2048]{1,0:T(8,128)(2,1)}, bf16[256,2048]{1,0:T(8,128)(2,1)}, u32[]{:S(2)}, u32[]{:S(2)}) collective-permute-start(bf16[256,2048]{1,0:T(8,128)(2,1)} %collective-permute-done.36.refs_7_), channel_id=1, source_target_pairs={{8,0},{16,8},{24,16},{28,24},{20,28},{12,20},{4,12},{0,4},{9,1},{1... | collective-permute-start | bytes 3145736 | tf_op jit(solution)/shard_map/ppermute | solution.py:89
  450.1 391.4 %reduce-scatter.6.cloned.1.call-start = ((), (), s32[]{:S(2)}) async-start(), calls=%async_computation.12 | async-start | bytes 20971520 | tf_op jit(solution)/shard_map/reduce_scatter | solution.py:612
  457.3 40.9 %collective-permute-start.38 = (bf16[256,2048]{1,0:T(8,128)(2,1)S(1)}, bf16[256,2048]{1,0:T(8,128)(2,1)}, u32[]{:S(2)}, u32[]{:S(2)}) collective-permute-start(bf16[256,2048]{1,0:T(8,128)(2,1)S(1)} %get-tuple-element.266), channel_id=1, source_target_pairs={{0,8},{8,16},{16,24},{24,28},{28,20},{20,12},{12,4},{4,0},{1,9},{9... | collective-permute-start | bytes 3145736 | tf_op jit(solution)/shard_map/ppermute | solution.py:123
  542.5 390.8 %reduce-scatter.8.cloned.1.call-start = ((), (), s32[]{:S(2)}) async-start(), calls=%async_computation.13 | async-start | bytes 20971520 | tf_op jit(solution)/shard_map/reduce_scatter | solution.py:612
  617.9 45.0 %collective-permute-start.46 = (bf16[256,2048]{1,0:T(8,128)(2,1)}, bf16[256,2048]{1,0:T(8,128)(2,1)}, u32[]{:S(2)}, u32[]{:S(2)}) collective-permute-start(bf16[256,2048]{1,0:T(8,128)(2,1)} %get-tuple-element.205), channel_id=1, source_target_pairs={{0,2},{1,3},{2,0},{3,1},{4,6},{5,7},{6,4},{7,5},{8,10},{9,11},{10,... | collective-permute-start | bytes 3145736 | tf_op jit(solution)/shard_map/ppermute | solution.py:152
  690.4 40.2 %collective-permute-start.51 = (bf16[256,2048]{1,0:T(8,128)(2,1)}, bf16[256,2048]{1,0:T(8,128)(2,1)}, u32[]{:S(2)}, u32[]{:S(2)}) collective-permute-start(bf16[256,2048]{1,0:T(8,128)(2,1)} %get-tuple-element.209), channel_id=1, source_target_pairs={{0,8},{8,16},{16,24},{24,28},{28,20},{20,12},{12,4},{4,0},{1,9},{9... | collective-permute-start | bytes 3145736 | tf_op jit(solution)/shard_map/ppermute | solution.py:123
  691.2 39.4 %collective-permute-start.52 = (bf16[256,2048]{1,0:T(8,128)(2,1)}, bf16[256,2048]{1,0:T(8,128)(2,1)}, u32[]{:S(2)}, u32[]{:S(2)}) collective-permute-start(bf16[256,2048]{1,0:T(8,128)(2,1)} %get-tuple-element.210), channel_id=1, source_target_pairs={{8,0},{16,8},{24,16},{28,24},{20,28},{12,20},{4,12},{0,4},{9,1},{1... | collective-permute-start | bytes 3145736 | tf_op jit(solution)/shard_map/ppermute | solution.py:119
  735.6 27.7 %collective-permute-start.53 = (bf16[256,2048]{1,0:T(8,128)(2,1)}, bf16[256,2048]{1,0:T(8,128)(2,1)}, u32[]{:S(2)}, u32[]{:S(2)}) collective-permute-start(bf16[256,2048]{1,0:T(8,128)(2,1)} %get-tuple-element.216), channel_id=1, source_target_pairs={{0,8},{8,16},{16,24},{24,28},{28,20},{20,12},{12,4},{4,0},{1,9},{9... | collective-permute-start | bytes 3145736 | tf_op jit(solution)/shard_map/ppermute | solution.py:123
  772.5 34.1 %collective-permute-start.61 = (bf16[256,2048]{1,0:T(8,128)(2,1)S(1)}, bf16[256,2048]{1,0:T(8,128)(2,1)S(1)}, u32[]{:S(2)}, u32[]{:S(2)}) collective-permute-start(bf16[256,2048]{1,0:T(8,128)(2,1)S(1)} %pad_maximum_fusion.4), channel_id=1, source_target_pairs={{8,0},{16,8},{24,16},{28,24},{20,28},{12,20},{4,12},{0,4},{9,1},{1... | collective-permute-start | bytes 3145736 | tf_op jit(solution)/shard_map/ppermute | solution.py:119
  819.4 60.6 %collective-permute-start.55 = (bf16[256,2048]{1,0:T(8,128)(2,1)}, bf16[256,2048]{1,0:T(8,128)(2,1)}, u32[]{:S(2)}, u32[]{:S(2)}) collective-permute-start(bf16[256,2048]{1,0:T(8,128)(2,1)} %get-tuple-element.277), channel_id=1, source_target_pairs={{0,1},{1,0},{2,3},{3,2},{4,5},{5,4},{6,7},{7,6},{8,9},{9,8},{10,11... | collective-permute-start | bytes 3145736 | tf_op jit(solution)/shard_map/ppermute | solution.py:180
  832.2 47.8 %collective-permute-start.57 = (bf16[256,2048]{1,0:T(8,128)(2,1)}, bf16[256,2048]{1,0:T(8,128)(2,1)S(1)}, u32[]{:S(2)}, u32[]{:S(2)}) collective-permute-start(bf16[256,2048]{1,0:T(8,128)(2,1)} %add_convert_fusion.6), channel_id=1, source_target_pairs={{0,2},{1,3},{2,0},{3,1},{4,6},{5,7},{6,4},{7,5},{8,10},{9,11},{10,... | collective-permute-start | bytes 3145736 | tf_op jit(solution)/shard_map/ppermute | solution.py:180
  841.5 49.0 %collective-permute-start.63 = (bf16[256,2048]{1,0:T(8,128)(2,1)}, bf16[256,2048]{1,0:T(8,128)(2,1)}, u32[]{:S(2)}, u32[]{:S(2)}) collective-permute-start(bf16[256,2048]{1,0:T(8,128)(2,1)} %add_convert_fusion.3), channel_id=1, source_target_pairs={{0,8},{8,16},{16,24},{24,28},{28,20},{20,12},{12,4},{4,0},{1,9},{9... | collective-permute-start | bytes 3145736 | tf_op jit(solution)/shard_map/ppermute | solution.py:123
  842.2 48.4 %collective-permute-start.64 = (bf16[256,2048]{1,0:T(8,128)(2,1)}, bf16[256,2048]{1,0:T(8,128)(2,1)}, u32[]{:S(2)}, u32[]{:S(2)}) collective-permute-start(bf16[256,2048]{1,0:T(8,128)(2,1)} %add_convert_fusion.1), channel_id=1, source_target_pairs={{8,0},{16,8},{24,16},{28,24},{20,28},{12,20},{4,12},{0,4},{9,1},{1... | collective-permute-start | bytes 3145736 | tf_op jit(solution)/shard_map/ppermute | solution.py:119
  (125 other events, 2160.6 us)
Sparse Core Ops, SparseCore 0:
  19.4 128.6 all-gather.3
  149.7 122.0 all-gather.5
  273.3 106.0 all-gather.7
  450.2 130.4 reduce-scatter.3
  583.3 148.5 reduce-scatter.5
  734.3 148.5 reduce-scatter.7
